TPU v7x, 128 devices: a whole 4x4x4 slice. The times are simulated.
128 devices in a mesh: seq: 32 (over x, y, core), head: 4 (over z).
Axes of the slice: x: 4, y: 4, z: 4, core: 2. Of those that a mesh axis runs over, the one named last changes fastest.
Arguments:
- layer_in: bfloat16 [16384, 2048], P('seq', 'head'), may hold values from -6 to 6
- gain1: float32 [2048], replicated, may hold values from 0.25 to 1.75
- wq: bfloat16 [2048, 2048], P(None, 'head'), may hold values from -0.125 to 0.125
- wk: bfloat16 [2048, 2048], P(None, 'head'), may hold values from -0.125 to 0.125
- wv: bfloat16 [2048, 4096], P(None, 'head'), may hold values from -0.125 to 0.125
- wg: bfloat16 [2048, 4096], P(None, 'head'), may hold values from -0.125 to 0.125
- wo: bfloat16 [4096, 2048], P('head'), may hold values from -0.125 to 0.125
- gain2: float32 [2048], replicated, may hold values from 0.25 to 1.75
- w1: bfloat16 [2048, 4096], P(None, 'head'), may hold values from -0.125 to 0.125
- w2: bfloat16 [4096, 2048], P('head'), may hold values from -0.125 to 0.125
- starts: int32 [3], replicated, may hold values from 0 to 16383, as said below
- cotangent: bfloat16 [16384, 2048], P('seq', 'head'), may hold values from -6 to 6
Outputs:
- out: bfloat16 [16384, 2048], P('seq', 'head')
- grad_x: float32 [16384, 2048], P('seq', 'head')
- grad_gain1: float32 [2048], P('head')
- grad_wq: float32 [2048, 2048], P('seq', 'head')
- grad_wk: float32 [2048, 2048], P('seq', 'head')
- grad_wv: float32 [2048, 4096], P('seq', 'head')
- grad_wg: float32 [2048, 4096], P('seq', 'head')
- grad_wo: float32 [4096, 2048], P('head', 'seq')
- grad_gain2: float32 [2048], P('head')
- grad_w1: float32 [2048, 4096], P('seq', 'head')
- grad_w2: float32 [4096, 2048], P('head', 'seq')
Inputs may be any that keep to these rules, and one draw needn't show every extreme that they name: starts[0] = 0 and the starts rise strictly; starts[1] and starts[2] each lie in the first 512 tokens or in the last 512 tokens, so that one document holds tokens of both.
All inputs are finite; a program needn't handle non-finite values.
Results may differ from a plain program's by a relative error of at most 0.023.
Values may be sent and summed in bfloat16 or wider, within the bound.
No kernel may reach another device: no remote copies, remote signals or barrier semaphores. Data moves between devices by JAX's collectives and lax.ppermute only.
A program may use at most 256 MiB of HBM per device.

v0:
```python
from functools import partial
import math

import jax
import jax.numpy as jnp
from jax import lax
from jax.sharding import PartitionSpec as P

KEY_DIM = 256
VALUE_DIM = 512


epsilon = 1e-05


def entering(x, axis, combine, identity, reverse):
    peers, position = (lax.axis_size(axis), lax.axis_index(axis))
    everything = jax.tree.map(lambda part: lax.all_gather(part, axis), x)
    start = jax.tree.map(
        lambda part, zero: jnp.broadcast_to(jnp.asarray(zero, part.dtype), part.shape), x, identity
    )

    def hop(k, before):
        at = peers - 1 - k if reverse else k
        reached = at > position if reverse else at < position
        new = combine(before, jax.tree.map(lambda part: part[at], everything))
        return jax.tree.map(lambda a, b: jnp.where(reached, a, b), new, before)

    return lax.fori_loop(0, peers, hop, start)


def carry_state(earlier, later_part):
    return (earlier[0] * later_part[0], earlier[1] * later_part[0][:, None, None] + later_part[1])


def split_parts(value_row_set):
    high_part = value_row_set.astype(jnp.bfloat16)
    return (high_part, (value_row_set - high_part.astype(jnp.float32)).astype(jnp.bfloat16))


def exact_contract(form, left, right):
    lefts = split_parts(left) if left.dtype == jnp.float32 else (left,)
    rights = split_parts(right) if right.dtype == jnp.float32 else (right,)
    total = jnp.einsum(form, lefts[0], rights[0], preferred_element_type=jnp.float32)
    if len(lefts) > 1:
        total = total + jnp.einsum(form, lefts[1], rights[0], preferred_element_type=jnp.float32)
    if len(rights) > 1:
        total = total + jnp.einsum(form, lefts[0], rights[1], preferred_element_type=jnp.float32)
    return total


def contract_rows(left, right):
    return lax.dot_general(
        left, right, (((0,), (0,)), ((), ())), preferred_element_type=jnp.float32
    )


def norm_forward(value_row_set):
    centered = value_row_set - jnp.mean(value_row_set, axis=-1, keepdims=True)
    inverse = lax.rsqrt(jnp.mean(centered * centered, axis=-1, keepdims=True) + epsilon)
    return (centered * inverse, inverse)


def norm_back(grad_shard, gain_shard, normed_shard, inverse, model_width):
    scaled = grad_shard * gain_shard
    first_sum, second_sum = lax.psum(
        (jnp.sum(scaled, axis=-1), jnp.sum(scaled * normed_shard, axis=-1)), "head"
    )
    return inverse * (
        scaled - first_sum[:, None] / model_width - normed_shard * second_sum[:, None] / model_width
    )


def rotate_pairs(value_row_set, cosine, sine_table, direction):
    half_dim = value_row_set.shape[-1] // 2
    first_part = value_row_set[..., :half_dim]
    second = value_row_set[..., half_dim:]
    return jnp.concatenate(
        [
            first_part * cosine - direction * second * sine_table,
            second * cosine + direction * first_part * sine_table,
        ],
        axis=-1,
    )


def shards(layer_in, gain1, wq, wk, wv, wg, wo, gain2, w1, w2, starts, cotangent):
    seq_rank = lax.axis_index("seq")
    head_rank = lax.axis_index("head")
    row_count, part_width = layer_in.shape
    model_width = part_width * lax.axis_size("head")
    local_heads = wq.shape[1] // KEY_DIM
    value_cols = wv.shape[1]
    col_start = head_rank * part_width
    gain1_part = lax.dynamic_slice_in_dim(gain1, col_start, part_width)
    gain2_part = lax.dynamic_slice_in_dim(gain2, col_start, part_width)
    group_floor = float(KEY_DIM)
    offsets = jnp.arange(row_count, dtype=jnp.int32)
    positions = seq_rank * row_count + offsets
    member = positions[:, None] >= starts[None, :]
    doc_ids = jnp.sum(member.astype(jnp.int32), axis=-1) - 1
    last_start = jnp.max(jnp.where(member, starts[None, :], 0), axis=-1)
    relative = (positions - last_start).astype(jnp.float32)
    prev_place = seq_rank * row_count - 1
    prior_doc = jnp.sum((prev_place >= starts).astype(jnp.int32)) - 1
    half_dim = KEY_DIM // 2
    frequency = jnp.exp(-math.log(10000.0) * jnp.arange(half_dim, dtype=jnp.float32) / half_dim)
    angles = relative[:, None] * frequency[None, :]
    cosine = jnp.cos(angles)[:, None, :]
    sine_table = jnp.sin(angles)[:, None, :]
    head_ids = (head_rank * local_heads + jnp.arange(local_heads, dtype=jnp.int32)).astype(
        jnp.float32
    )
    log_decay = jnp.log1p(-jnp.exp2(-5.0 - head_ids))
    gap_grid = offsets[:, None] - offsets[None, :]
    causal = gap_grid >= 0
    keep_mask = causal & (doc_ids[:, None] == doc_ids[None, :])
    gap_float = jnp.where(causal, gap_grid, 0).astype(jnp.float32)
    decay_grid = jnp.where(
        keep_mask[None], jnp.exp(gap_float[None] * log_decay[:, None, None]), 0.0
    )
    step_float = offsets.astype(jnp.float32)
    arrival_decay = (
        jnp.exp((step_float[None, :] + 1.0) * log_decay[:, None])
        * (doc_ids == prior_doc).astype(jnp.float32)[None, :]
    )
    last_doc = doc_ids[row_count - 1]
    departure_decay = (
        jnp.exp((row_count - 1.0 - step_float)[None, :] * log_decay[:, None])
        * (doc_ids == last_doc).astype(jnp.float32)[None, :]
    )
    segment_decay = jnp.exp(row_count * log_decay) * (last_doc == prior_doc).astype(jnp.float32)
    arrival_columns = arrival_decay.T[:, :, None]
    departure_columns = departure_decay.T[:, :, None]
    whole_rows = lax.all_gather(layer_in, "head", axis=1, tiled=True).astype(jnp.float32)
    normed1, inverse1 = norm_forward(whole_rows)
    norm_low = (normed1 * gain1).astype(jnp.bfloat16)
    query_pre = jnp.dot(norm_low, wq, preferred_element_type=jnp.float32).reshape(
        row_count, local_heads, KEY_DIM
    )
    query_rows = rotate_pairs(query_pre, cosine, sine_table, 1.0).astype(jnp.bfloat16)
    key_pre = jnp.dot(norm_low, wk, preferred_element_type=jnp.float32).reshape(
        row_count, local_heads, KEY_DIM
    )
    key_row_set = rotate_pairs(key_pre, cosine, sine_table, 1.0).astype(jnp.bfloat16)
    value_row_set = (
        jnp.dot(norm_low, wv, preferred_element_type=jnp.float32)
        .astype(jnp.bfloat16)
        .reshape(row_count, local_heads, VALUE_DIM)
    )
    gate_pre = jnp.dot(norm_low, wg, preferred_element_type=jnp.float32)
    scores = jnp.einsum("thk,shk->hts", query_rows, key_row_set, preferred_element_type=jnp.float32)
    weighted = scores * decay_grid
    within_segment_part = exact_contract("hts,shv->thv", weighted, value_row_set)
    segment_state = exact_contract(
        "aqc,aqr->qcr", key_row_set.astype(jnp.float32) * departure_columns, value_row_set
    )
    identity = (jnp.ones((local_heads,), jnp.float32), jnp.zeros_like(segment_state))
    _, incoming_state = entering(
        (segment_decay, segment_state), "seq", carry_state, identity, False
    )
    retention_output = within_segment_part + arrival_columns * exact_contract(
        "mfw,fwq->mfq", query_rows, incoming_state
    )
    centered = retention_output - jnp.mean(retention_output, axis=-1, keepdims=True)
    group_inv = lax.rsqrt(jnp.mean(centered * centered, axis=-1, keepdims=True) + group_floor)
    grouped = centered * group_inv
    flat_group = grouped.reshape(row_count, value_cols)
    swish_gate = jax.nn.silu(gate_pre)
    mixed = (flat_group * swish_gate).astype(jnp.bfloat16)
    branch = lax.psum(
        jnp.dot(mixed, wo, preferred_element_type=jnp.float32).astype(jnp.bfloat16), "head"
    ).astype(jnp.float32)
    middle = whole_rows + branch
    normed2, inverse2 = norm_forward(middle)
    ffn_input = (normed2 * gain2).astype(jnp.bfloat16)
    hidden_pre = jnp.dot(ffn_input, w1, preferred_element_type=jnp.float32)
    hidden = jax.nn.gelu(hidden_pre, approximate=False).astype(jnp.bfloat16)
    ffn_part = lax.psum_scatter(
        jnp.dot(hidden, w2, preferred_element_type=jnp.float32).astype(jnp.bfloat16),
        "head",
        scatter_dimension=1,
        tiled=True,
    ).astype(jnp.float32)
    middle_part = lax.dynamic_slice_in_dim(middle, col_start, part_width, 1)
    output = (middle_part + ffn_part).astype(jnp.bfloat16)
    grad_out = cotangent.astype(jnp.float32)
    grad_full = lax.all_gather(cotangent, "head", axis=1, tiled=True)
    grad_hidden = jnp.dot(grad_full, w2.T, preferred_element_type=jnp.float32)
    _, gelu_back = jax.vjp(partial(jax.nn.gelu, approximate=False), hidden_pre)
    grad_pre = gelu_back(grad_hidden)[0].astype(jnp.bfloat16)
    grad_ffn_in = lax.psum_scatter(
        jnp.dot(grad_pre, w1.T, preferred_element_type=jnp.float32).astype(jnp.bfloat16),
        "head",
        scatter_dimension=1,
        tiled=True,
    ).astype(jnp.float32)
    normed2_part = lax.dynamic_slice_in_dim(normed2, col_start, part_width, 1)
    gain2_grad = jnp.sum(grad_ffn_in * normed2_part, axis=0)
    grad_middle = grad_out + norm_back(grad_ffn_in, gain2_part, normed2_part, inverse2, model_width)
    grad_branch = lax.all_gather(grad_middle.astype(jnp.bfloat16), "head", axis=1, tiled=True)
    grad_mixed = jnp.dot(grad_branch, wo.T, preferred_element_type=jnp.float32)
    _, silu_back = jax.vjp(jax.nn.silu, gate_pre)
    grad_gate = silu_back(grad_mixed * flat_group)[0].astype(jnp.bfloat16)
    grad_group = (grad_mixed * swish_gate).reshape(row_count, local_heads, VALUE_DIM)
    retention_gradient = group_inv * (
        grad_group
        - jnp.mean(grad_group, axis=-1, keepdims=True)
        - grouped * jnp.mean(grad_group * grouped, axis=-1, keepdims=True)
    )
    grad_scores = exact_contract("thv,shv->hts", retention_gradient, value_row_set) * decay_grid
    segment_own_state = exact_contract(
        "pos,pob->osb", query_rows, retention_gradient * arrival_columns
    )
    _, outgoing_state = entering(
        (segment_decay, segment_own_state), "seq", carry_state, identity, True
    )
    grad_query = exact_contract(
        "hts,shk->thk", grad_scores, key_row_set
    ) + arrival_columns * exact_contract("lws,wbs->lwb", retention_gradient, incoming_state)
    grad_key = exact_contract(
        "hts,thk->shk", grad_scores, query_rows
    ) + departure_columns * exact_contract("yab,adb->yad", value_row_set, outgoing_state)
    grad_value = exact_contract(
        "hts,thv->shv", weighted, retention_gradient
    ) + departure_columns * exact_contract("buo,uof->buf", key_row_set, outgoing_state)
    grad_qpre = (
        rotate_pairs(grad_query, cosine, sine_table, -1.0)
        .reshape(row_count, -1)
        .astype(jnp.bfloat16)
    )
    grad_kpre = (
        rotate_pairs(grad_key, cosine, sine_table, -1.0).reshape(row_count, -1).astype(jnp.bfloat16)
    )
    grad_vpre = grad_value.reshape(row_count, -1).astype(jnp.bfloat16)
    back_terms = (
        jnp.dot(grad_qpre, wq.T, preferred_element_type=jnp.float32)
        + jnp.dot(grad_kpre, wk.T, preferred_element_type=jnp.float32)
        + jnp.dot(grad_vpre, wv.T, preferred_element_type=jnp.float32)
        + jnp.dot(grad_gate, wg.T, preferred_element_type=jnp.float32)
    )
    grad_norm_in = lax.psum_scatter(
        back_terms.astype(jnp.bfloat16), "head", scatter_dimension=1, tiled=True
    ).astype(jnp.float32)
    normed1_part = lax.dynamic_slice_in_dim(normed1, col_start, part_width, 1)
    gain1_grad = jnp.sum(grad_norm_in * normed1_part, axis=0)
    grad_x = grad_middle + norm_back(grad_norm_in, gain1_part, normed1_part, inverse1, model_width)
    gain_totals = lax.psum((gain1_grad, gain2_grad), "seq")
    summed = (
        lax.psum_scatter(
            contract_rows(norm_low, grad_qpre).astype(jnp.bfloat16),
            "seq",
            scatter_dimension=0,
            tiled=True,
        ).astype(jnp.float32),
        lax.psum_scatter(
            contract_rows(norm_low, grad_kpre).astype(jnp.bfloat16),
            "seq",
            scatter_dimension=0,
            tiled=True,
        ).astype(jnp.float32),
        lax.psum_scatter(
            contract_rows(norm_low, grad_vpre).astype(jnp.bfloat16),
            "seq",
            scatter_dimension=0,
            tiled=True,
        ).astype(jnp.float32),
        lax.psum_scatter(
            contract_rows(norm_low, grad_gate).astype(jnp.bfloat16),
            "seq",
            scatter_dimension=0,
            tiled=True,
        ).astype(jnp.float32),
        lax.psum_scatter(
            contract_rows(mixed, grad_branch).astype(jnp.bfloat16),
            "seq",
            scatter_dimension=1,
            tiled=True,
        ).astype(jnp.float32),
        lax.psum_scatter(
            contract_rows(ffn_input, grad_pre).astype(jnp.bfloat16),
            "seq",
            scatter_dimension=0,
            tiled=True,
        ).astype(jnp.float32),
        lax.psum_scatter(
            contract_rows(hidden, grad_full).astype(jnp.bfloat16),
            "seq",
            scatter_dimension=1,
            tiled=True,
        ).astype(jnp.float32),
    )
    return (
        output,
        grad_x,
        gain_totals[0],
        summed[0],
        summed[1],
        summed[2],
        summed[3],
        summed[4],
        gain_totals[1],
        summed[5],
        summed[6],
    )


def solution(mesh):
    return jax.shard_map(
        shards,
        mesh=mesh,
        in_specs=(
            P("seq", "head"),
            P(),
            P(None, "head"),
            P(None, "head"),
            P(None, "head"),
            P(None, "head"),
            P("head", None),
            P(),
            P(None, "head"),
            P("head", None),
            P(),
            P("seq", "head"),
        ),
        out_specs=(
            P("seq", "head"),
            P("seq", "head"),
            P("head"),
            P("seq", "head"),
            P("seq", "head"),
            P("seq", "head"),
            P("seq", "head"),
            P("head", "seq"),
            P("head"),
            P("seq", "head"),
            P("head", "seq"),
        ),
        check_vma=False,
    )
```

profile of v0, /device:TPU:0, one launch (start us, length us, event | category | flops | bytes accessed | tf_op | source)
XLA Modules:
  0.0 1231.1 jit_solution(2510656587237201382)
XLA Ops:
  13.9 29.4 %all-gather.9.cloned.1.call-done = bf16[512,2048]{1,0:T(8,128)(2,1)} async-done(((bf16[512,512]{1,0:T(8,128)(2,1)}), bf16[512,2048]{1,0:T(8,128)(2,1)}) %all-gather.9.cloned.1.call-update) | async-done | bytes 2097168 | tf_op jit(solution)/shard_map/all_gather | solution.py:135
  69.9 21.7 %all-gather.2 = f32[32,1,2]{2,1,0:T(1,128)S(1)} all-gather(f32[1,1,2]{2,1,0:T(1,128)S(1)} %multiply_bitcast_fusion), channel_id=1, replica_groups=mesh['seq'=32,'head'=4] {'seq'}, dimensions={0}, use_global_device_ids=true | all-gather | bytes 264 | tf_op jit(solution)/shard_map/all_gather | solution.py:18
  99.5 83.3 %all-gather.15.cloned.1.call-done = f32[64,256,512]{2,1,0:T(8,128)} async-done(((f32[2,256,512]{2,1,0:T(8,128)}), f32[64,256,512]{2,1,0:T(8,128)}) %all-gather.15.cloned.1.call-update) | async-done | bytes 33554448 | tf_op jit(solution)/shard_map/all_gather | solution.py:18
  182.8 53.1 %while.30 = (s32[]{:T(128)}, f32[2,256,512]{2,1,0:T(8,128)S(1)}, s32[]{:T(128)}, f32[32,2]{1,0:T(8,128)S(1)}, f32[32,2,256,512]{3,2,1,0:T(8,128)}, /*index=5*/s32[]{:T(128)}, s32[]{:T(128)}) while((s32[]{:T(128)}, f32[2,256,512]{2,1,0:T(8,128)S(1)}, s32[]{:T(128)}, f32[32,2]{1,0:T(8,128)S(1)}, f32[32,2,256,512]{3,2,1,0:T(8,128)}, ...), condition=%wide.region_6.7_spmd.clone, body=%wide.region_5.6_spmd.clone.sunk | while | flops 1048580 | bytes 3145865 | solution.py:29
  245.1 7.5 multiply_convert_fusion.3
  258.4 57.4 %all-reduce.5.cloned.1.call-done = bf16[512,2048]{1,0:T(8,128)(2,1)} async-done(((bf16[512,2048]{1,0:T(8,128)(2,1)}), bf16[512,2048]{1,0:T(8,128)(2,1)}) %all-reduce.5.cloned.1.call-update) | async-done | bytes 2097168 | tf_op jit(solution)/shard_map/psum | solution.py:171
  328.9 19.3 %all-gather.11.cloned.1.call-done = bf16[512,2048]{1,0:T(8,128)(2,1)} async-done(((bf16[512,512]{1,0:T(8,128)(2,1)}), bf16[512,2048]{1,0:T(8,128)(2,1)}) %all-gather.11.cloned.1.call-update) | async-done | bytes 2097168 | tf_op jit(solution)/shard_map/all_gather | solution.py:188
  348.2 10.7 add_convert_fusion.1
  363.8 29.8 %reduce-scatter.13.cloned.1.call-done = bf16[512,512]{1,0:T(8,128)(2,1)} async-done(((bf16[512,2048]{1,0:T(8,128)(2,1)}), bf16[512,512]{1,0:T(8,128)(2,1)}) %reduce-scatter.13.cloned.1.call-update) | async-done | bytes 524304 | tf_op jit(solution)/shard_map/reduce_scatter | solution.py:192
  395.4 8.5 all-reduce.2
  406.9 30.4 %all-gather.13.cloned.1.call-done = bf16[512,2048]{1,0:T(8,128)(2,1)} async-done(((bf16[512,512]{1,0:T(8,128)(2,1)}), bf16[512,2048]{1,0:T(8,128)(2,1)}) %all-gather.13.cloned.1.call-update) | async-done | bytes 2097168 | tf_op jit(solution)/shard_map/all_gather | solution.py:201
  437.2 8.7 fusion.70
  470.8 6.9 convolution_convert_fusion.1
  500.3 69.9 %all-gather.17.cloned.1.call-done = f32[64,256,512]{2,1,0:T(8,128)} async-done(((f32[2,256,512]{2,1,0:T(8,128)}), f32[64,256,512]{2,1,0:T(8,128)}) %all-gather.17.cloned.1.call-update) | async-done | bytes 33554448 | tf_op jit(solution)/shard_map/all_gather | solution.py:18
  570.2 53.8 %while.31 = (s32[]{:T(128)}, f32[2,256,512]{2,1,0:T(8,128)S(1)}, s32[]{:T(128)}, f32[32,2]{1,0:T(8,128)S(1)}, f32[32,2,256,512]{3,2,1,0:T(8,128)}, /*index=5*/s32[]{:T(128)}, s32[]{:T(128)}, s32[]{:T(128)}, s32[]{:T(128)}) while((s32[]{:T(128)}, f32[2,256,512]{2,1,0:T(8,128)S(1)}, s32[]{:T(128)}, f32[32,2]{1,0:T(8,128)S(1)}, ...), condition=%wide.region_21.22_spmd.clone, body=%wide.region_20.21_spmd.clone.sunk | while | flops 1048584 | bytes 3145927 | solution.py:29
  678.8 8.5 reduce-scatter.29.cloned.1.call-done
  689.0 83.1 %reduce-scatter.27.cloned.1.call-done = bf16[64,1024]{1,0:T(8,128)(2,1)} async-done(((bf16[2048,1024]{1,0:T(8,128)(2,1)}), bf16[64,1024]{1,0:T(8,128)(2,1)}) %reduce-scatter.27.cloned.1.call-update) | async-done | bytes 131088 | tf_op jit(solution)/shard_map/reduce_scatter | solution.py:280
  773.7 83.7 %reduce-scatter.25.cloned.1.call-done = bf16[1024,64]{0,1:T(8,128)(2,1)} async-done(((bf16[1024,2048]{0,1:T(8,128)(2,1)}), bf16[1024,64]{0,1:T(8,128)(2,1)}) %reduce-scatter.25.cloned.1.call-update) | async-done | bytes 131088 | tf_op jit(solution)/shard_map/reduce_scatter | solution.py:274
  859.0 83.0 %reduce-scatter.23.cloned.1.call-done = bf16[64,1024]{1,0:T(8,128)(2,1)} async-done(((bf16[2048,1024]{1,0:T(8,128)(2,1)}), bf16[64,1024]{1,0:T(8,128)(2,1)}) %reduce-scatter.23.cloned.1.call-update) | async-done | bytes 131088 | tf_op jit(solution)/shard_map/reduce_scatter | solution.py:268
  943.6 80.5 %reduce-scatter.17.cloned.1.call-done = bf16[64,512]{1,0:T(8,128)(2,1)} async-done(((bf16[2048,512]{1,0:T(8,128)(2,1)}), bf16[64,512]{1,0:T(8,128)(2,1)}) %reduce-scatter.17.cloned.1.call-update) | async-done | bytes 65552 | tf_op jit(solution)/shard_map/reduce_scatter | solution.py:250
  1025.6 80.5 %reduce-scatter.19.cloned.1.call-done = bf16[64,512]{1,0:T(8,128)(2,1)} async-done(((bf16[2048,512]{1,0:T(8,128)(2,1)}), bf16[64,512]{1,0:T(8,128)(2,1)}) %reduce-scatter.19.cloned.1.call-update) | async-done | bytes 65552 | tf_op jit(solution)/shard_map/reduce_scatter | solution.py:256
  1107.5 30.2 %reduce-scatter.15.cloned.1.call-done = bf16[512,512]{1,0:T(8,128)(2,1)} async-done(((bf16[512,2048]{1,0:T(8,128)(2,1)}), bf16[512,512]{1,0:T(8,128)(2,1)}) %reduce-scatter.15.cloned.1.call-update) | async-done | bytes 524304 | tf_op jit(solution)/shard_map/reduce_scatter | solution.py:242
  1139.6 67.8 %all-reduce = (f32[512]{0:T(512)}, f32[512]{0:T(512)}) all-reduce(f32[512]{0:T(512)S(1)} %get-tuple-element.317, f32[512]{0:T(512)S(1)} %get-tuple-element.315), channel_id=1, replica_groups=mesh['seq'=32,'head'=4] {'seq'}, use_global_device_ids=true, to_apply=%region_28.29 | all-reduce | flops 1024 | bytes 8192 | tf_op jit(solution)/shard_map/psum | solution.py:248
  1207.4 8.3 all-reduce.1
  (407 shorter events, 303.4 us)
Async XLA Ops:
  7.2 46.3 %copy-start = (bf16[2048,512]{1,0:T(8,128)(2,1)S(1)}, bf16[2048,512]{1,0:T(8,128)(2,1)}, u32[]{:S(2)}) copy-start(bf16[2048,512]{1,0:T(8,128)(2,1)} %param.18) | copy-start | bytes 6291460
  7.2 36.1 %all-gather.9.cloned.1.call-start = ((), (), s32[]{:S(2)}) async-start(), calls=%async_computation.10 | async-start | bytes 2621440 | tf_op jit(solution)/shard_map/all_gather | solution.py:135
  7.9 174.9 %all-gather.15.cloned.1.call-start = ((), (), s32[]{:S(2)}) async-start(), calls=%async_computation.24 | async-start | bytes 34603008 | tf_op jit(solution)/shard_map/all_gather | solution.py:18
  13.9 51.7 %copy-start.38 = (f32[512,128]{1,0:T(8,128)}, f32[512,128]{1,0:T(8,128)S(1)}, u32[]{:S(2)}) copy-start(f32[512,128]{1,0:T(8,128)S(1)} %get-tuple-element.380) | copy-start | bytes 786436
  69.1 246.7 %all-reduce.5.cloned.1.call-start = ((), (), s32[]{:S(2)}) async-start(), calls=%async_computation.11 | async-start | bytes 4194304 | tf_op jit(solution)/shard_map/psum | solution.py:171
  245.1 8.5 copy-start.62
  257.4 90.8 %all-gather.11.cloned.1.call-start = ((), (), s32[]{:S(2)}) async-start(), calls=%async_computation.13 | async-start | bytes 2621440 | tf_op jit(solution)/shard_map/all_gather | solution.py:188
  257.9 135.7 %reduce-scatter.13.cloned.1.call-start = ((), (), s32[]{:S(2)}) async-start(), calls=%async_computation.14 | async-start | bytes 2621440 | tf_op jit(solution)/shard_map/reduce_scatter | solution.py:192
  348.2 11.7 copy-start.61
  363.7 73.5 %all-gather.13.cloned.1.call-start = ((), (), s32[]{:S(2)}) async-start(), calls=%async_computation.15 | async-start | bytes 2621440 | tf_op jit(solution)/shard_map/all_gather | solution.py:201
  406.7 163.5 %all-gather.17.cloned.1.call-start = ((), (), s32[]{:S(2)}) async-start(), calls=%async_computation.25 | async-start | bytes 34603008 | tf_op jit(solution)/shard_map/all_gather | solution.py:18
  456.5 220.0 %reduce-scatter.11.cloned.1.call-start = ((), (), s32[]{:S(2)}) async-start(), calls=%async_computation.12 | async-start | bytes 2621440 | tf_op jit(solution)/shard_map/reduce_scatter | solution.py:179
  464.2 223.2 %reduce-scatter.29.cloned.1.call-start = ((), (), s32[]{:S(2)}) async-start(), calls=%async_computation.23 | async-start | bytes 4325376 | tf_op jit(solution)/shard_map/reduce_scatter | solution.py:286
  470.7 301.3 %reduce-scatter.27.cloned.1.call-start = ((), (), s32[]{:S(2)}) async-start(), calls=%async_computation.22 | async-start | bytes 4325376 | tf_op jit(solution)/shard_map/reduce_scatter | solution.py:280
  477.7 379.6 %reduce-scatter.25.cloned.1.call-start = ((), (), s32[]{:S(2)}) async-start(), calls=%async_computation.21 | async-start | bytes 4325376 | tf_op jit(solution)/shard_map/reduce_scatter | solution.py:274
  484.1 457.9 %reduce-scatter.23.cloned.1.call-start = ((), (), s32[]{:S(2)}) async-start(), calls=%async_computation.20 | async-start | bytes 4325376 | tf_op jit(solution)/shard_map/reduce_scatter | solution.py:268
  500.2 69.9 %copy-start.1 = (f32[2,256,512]{2,1,0:T(8,128)S(1)}, f32[2,256,512]{2,1,0:T(8,128)}, u32[]{:S(2)}) copy-start(f32[2,256,512]{2,1,0:T(8,128)} %custom-call.1) | copy-start | bytes 3145732
  500.3 523.8 %reduce-scatter.17.cloned.1.call-start = ((), (), s32[]{:S(2)}) async-start(), calls=%async_computation.17 | async-start | bytes 2162688 | tf_op jit(solution)/shard_map/reduce_scatter | solution.py:250
  635.6 470.4 %reduce-scatter.19.cloned.1.call-start = ((), (), s32[]{:S(2)}) async-start(), calls=%async_computation.18 | async-start | bytes 2162688 | tf_op jit(solution)/shard_map/reduce_scatter | solution.py:256
  651.6 486.2 %reduce-scatter.15.cloned.1.call-start = ((), (), s32[]{:S(2)}) async-start(), calls=%async_computation.16 | async-start | bytes 2621440 | tf_op jit(solution)/shard_map/reduce_scatter | solution.py:242
  668.5 554.1 %reduce-scatter.21.cloned.1.call-start = ((), (), s32[]{:S(2)}) async-start(), calls=%async_computation.19 | async-start | bytes 4325376 | tf_op jit(solution)/shard_map/reduce_scatter | solution.py:262
  678.8 536.9 %copy-start.31 = (bf16[512,512]{1,0:T(8,128)(2,1)S(1)}, bf16[512,512]{1,0:T(8,128)(2,1)}, u32[]{:S(2)}) copy-start(bf16[512,512]{1,0:T(8,128)(2,1)} %param.27) | copy-start | bytes 1572868
  678.8 536.9 %copy-start.32 = (bf16[512,512]{1,0:T(8,128)(2,1)S(1)}, bf16[512,512]{1,0:T(8,128)(2,1)}, u32[]{:S(2)}) copy-start(bf16[512,512]{1,0:T(8,128)(2,1)} %reduce-scatter.13.cloned.1.call-done) | copy-start | bytes 1572868
  678.8 536.9 %copy-start.57 = (f32[512]{0:T(512)S(1)}, f32[512]{0:T(512)}, u32[]{:S(2)}) copy-start(f32[512]{0:T(512)} %copy-done.56) | copy-start | bytes 6148
  (60 other events, 143.4 us)
Sparse Core Ops, SparseCore 0:
  9.7 33.5 all-gather.8
  69.2 113.5 all-gather.14
  257.5 58.3 all-reduce.4
  317.5 30.6 all-gather.10
  363.8 29.7 reduce-scatter.12
  406.8 30.4 all-gather.12
  456.6 113.5 all-gather.16
  572.6 29.2 reduce-scatter.10
  605.9 81.3 reduce-scatter.28
  690.8 81.1 reduce-scatter.26
  776.1 81.1 reduce-scatter.24
  860.9 81.0 reduce-scatter.22
  946.0 78.0 reduce-scatter.16
  1027.9 78.1 reduce-scatter.18
  1108.4 29.3 reduce-scatter.14
  1141.3 81.3 reduce-scatter.20
where the time goes:
time: 1240 us; the launch traced here: 1230 us
  waiting for transfers between devices  774 us (62%)
  other arithmetic  158 us (13%)
  matrix products  138 us (11%)
  blocking collectives  106 us (9%)
  local copies, waits for them, and re-layouts  34.7 us (3%)
  between operations  16.3 us (1%)
    all_gather x2, waiting for transfers between devices, entering(): everything = jax.tree.map(lambda part: lax.all_gather(part, axis), x)  153 us
    select_n x64, other arithmetic, hop(): return jax.tree.map(lambda a, b: jnp.where(reached, a, b), new, before)  104 us
    reduce_scatter x1, waiting for transfers between devices, shards(): lax.psum_scatter(contract_rows(mixed, grad_branch).astype(jnp.bfloat16),...  83.7 us
    reduce_scatter x1, waiting for transfers between devices, shards(): lax.psum_scatter(contract_rows(ffn_input, grad_pre).astype(jnp.bfloat16),...  83.1 us
    reduce_scatter x1, waiting for transfers between devices, shards(): lax.psum_scatter(contract_rows(norm_low, grad_gate).astype(jnp.bfloat16),...  83 us
    reduce_scatter x1, waiting for transfers between devices, shards(): lax.psum_scatter(contract_rows(norm_low, grad_kpre).astype(jnp.bfloat16),...  80.5 us
    reduce_scatter x1, waiting for transfers between devices, shards(): lax.psum_scatter(contract_rows(norm_low, grad_qpre).astype(jnp.bfloat16),...  80.5 us
    psum x1, blocking collectives, shards(): gain_totals = lax.psum((gain1_grad, gain2_grad), 'seq')  67.8 us
  transfers between devices with their start and end apart: 16, of which 15 were waited for; matrix products, arithmetic and copies ran while one was open for 14% of the time, Pallas kernels for 0%

commit v1 on v0

v1 whole, which is shorter than its diff:
```python
from functools import partial
import math

import jax
import jax.numpy as jnp
from jax import lax
from jax.sharding import PartitionSpec as P

KEY_DIM = 256
VALUE_DIM = 512
SIDE = 4
CORES = 2
EPSILON = 1e-05
F32 = jnp.float32
BF16 = jnp.bfloat16


def head_shift(step):
    return [(h, (h + step) % SIDE) for h in range(SIDE)]


def seq_index(x, y, core):
    return (x * SIDE + y) * CORES + core


def seq_shift(dx, dy, swap=0):
    return [
        (seq_index(x, y, core), seq_index((x + dx) % SIDE, (y + dy) % SIDE, core ^ swap))
        for x in range(SIDE)
        for y in range(SIDE)
        for core in range(CORES)
    ]


def dot(left, right):
    return jnp.dot(left, right, preferred_element_type=F32)


def dot_t(left, right):
    return lax.dot_general(left, right, (((1,), (1,)), ((), ())), preferred_element_type=F32)


def einsum(form, left, right):
    return jnp.einsum(form, left.astype(BF16), right.astype(BF16), preferred_element_type=F32)


def after(value, *others):
    return lax.optimization_barrier((value, *others))[0]


def gather_parts(block):
    return [block] + [lax.ppermute(block, "head", head_shift(k)) for k in (1, 3, 2)]


def assemble(parts, head_rank):
    rows, width = parts[0].shape
    whole = jnp.zeros((rows, SIDE * width), parts[0].dtype)
    for part, k in zip(parts, (0, 1, 3, 2)):
        at = lax.rem(head_rank + SIDE - k, SIDE)
        whole = lax.dynamic_update_slice(whole, part, (0, at * width))
    return whole


def scatter_cols(partial_sum, head_rank):
    width = partial_sum.shape[1] // SIDE

    def block(k):
        at = lax.rem(head_rank + k, SIDE)
        return lax.dynamic_slice_in_dim(partial_sum, at * width, width, 1)

    received = [lax.ppermute(block(k), "head", head_shift(k)) for k in (2, 1, 3)]
    total = block(0).astype(F32)
    for piece in received:
        total = total + piece.astype(F32)
    return total


def sum_heads(values):
    total = values
    for k in (1, 2, 3):
        total = total + lax.ppermute(values, "head", head_shift(k))
    return total


def axis_phase(blocks, dim, position, shift_of):
    def block(k):
        return lax.dynamic_index_in_dim(blocks, lax.rem(position + k, SIDE), dim, False)

    received = [lax.ppermute(block(k), "seq", shift_of(k)) for k in (2, 1, 3)]
    total = block(0).astype(F32)
    for piece in received:
        total = total + piece.astype(F32)
    return total


def weight_scatter(left_halves, right, place, x_first):
    x, y, core = place
    left_own, left_other = left_halves
    width = right.shape[1]
    other = dot(left_other, right).astype(BF16)
    arrived = lax.ppermute(other, "seq", seq_shift(0, 0, 1))
    own = (dot(left_own, right) + arrived.astype(F32)).astype(BF16)
    own = own.reshape(SIDE, SIDE, -1, width)
    x_of = lambda k: seq_shift(k, 0)
    y_of = lambda k: seq_shift(0, k)
    if x_first:
        half = axis_phase(own, 0, x, x_of).astype(BF16)
        return axis_phase(half, 0, y, y_of)
    half = axis_phase(own, 1, y, y_of).astype(BF16)
    return axis_phase(half, 0, x, x_of)


def state_scan(state, decay, place, reverse):
    x, y, core = place
    swap = seq_shift(0, 0, 1)
    keys, values = state.shape[1:]
    own = lax.dynamic_index_in_dim(state, core, 0, False)
    give = lax.dynamic_index_in_dim(state, 1 - core, 0, False).astype(BF16)
    got = lax.ppermute(give, "seq", swap).astype(F32)
    own_decay = lax.dynamic_index_in_dim(decay, core, 0, False)
    far_core = (core == 0) if not reverse else (core == 1)
    chip_decay = own_decay * own_decay
    total = jnp.where(far_core, own_decay * own + got, own + own_decay * got)
    quarters = total.astype(BF16).reshape(SIDE, keys // SIDE, values)
    row = {}
    for k in (0, 1, 3, 2):
        piece = lax.dynamic_index_in_dim(quarters, lax.rem(y + k, SIDE), 0, False)
        row[k] = piece if k == 0 else lax.ppermute(piece, "seq", seq_shift(0, k))
    pieces = jnp.stack([row[k].astype(F32) for k in range(SIDE)])
    origin = lax.rem(y - jnp.arange(SIDE) + SIDE, SIDE)
    towards = origin if reverse else SIDE - 1 - origin
    row_weight = jnp.exp(jnp.log(chip_decay) * towards.astype(F32))
    row_total = jnp.sum(row_weight[:, None, None] * pieces, axis=0).astype(BF16)
    row_decay = chip_decay**SIDE
    before = jnp.zeros_like(row_total, F32)
    for k in (1, 3, 2):
        piece = lax.ppermute(row_total, "seq", seq_shift(k, 0)).astype(F32)
        if reverse:
            hops = SIDE - k
            counts = x + hops < SIDE
        else:
            hops = k
            counts = x >= k
        before = before + jnp.where(counts, row_decay ** (hops - 1), 0.0) * piece
    targets = jnp.arange(SIDE)
    if reverse:
        gap = origin[None, :] - targets[:, None]
        carry = SIDE - 1 - targets
    else:
        gap = targets[:, None] - origin[None, :]
        carry = targets
    weights = jnp.where(gap > 0, jnp.exp(jnp.log(chip_decay) * (gap - 1).astype(F32)), 0.0)
    carry_weight = jnp.exp(jnp.log(chip_decay) * carry.astype(F32))
    answers = (
        jnp.einsum("tk,kab->tab", weights, pieces, precision=lax.Precision.HIGHEST)
        + carry_weight[:, None, None] * before[None]
    ).astype(BF16)
    back = [None] * SIDE
    for k in (0, 1, 3, 2):
        at = lax.rem(y + k, SIDE)
        piece = lax.dynamic_index_in_dim(answers, at, 0, False)
        back[k] = piece if k == 0 else lax.ppermute(piece, "seq", seq_shift(0, k))
    chip_in = jnp.zeros((SIDE, keys // SIDE, values), BF16)
    for k in range(SIDE):
        at = lax.rem(y - k + SIDE, SIDE)
        chip_in = lax.dynamic_update_index_in_dim(chip_in, back[k], at, 0)
    chip_in = chip_in.reshape(keys, values).astype(F32)
    later = own_decay * chip_in + jnp.where(far_core, own, got)
    mine = jnp.where(far_core, chip_in, later)
    theirs = jnp.where(far_core, later, chip_in).astype(BF16)
    from_sibling = lax.ppermute(theirs, "seq", swap)
    mine = mine.astype(BF16)
    first = jnp.where(core == 0, mine, from_sibling)
    second = jnp.where(core == 0, from_sibling, mine)
    return jnp.stack([first, second])


def norm_forward(rows):
    centered = rows - jnp.mean(rows, axis=-1, keepdims=True)
    inverse = lax.rsqrt(jnp.mean(centered * centered, axis=-1, keepdims=True) + EPSILON)
    return (centered * inverse, inverse)


def rotate_pairs(rows, cosine, sine, direction):
    half = rows.shape[-1] // 2
    first = rows[..., :half]
    second = rows[..., half:]
    return jnp.concatenate(
        [
            first * cosine - direction * second * sine,
            second * cosine + direction * first * sine,
        ],
        axis=-1,
    )


def shards(layer_in, gain1, wq, wk, wv, wg, wo, gain2, w1, w2, starts, cotangent):
    seq_rank = lax.axis_index("seq")
    head_rank = lax.axis_index("head")
    place = (seq_rank // (SIDE * CORES), (seq_rank // CORES) % SIDE, seq_rank % CORES)
    core = place[2]
    rows, width = layer_in.shape
    model = width * SIDE
    heads = wq.shape[1] // KEY_DIM
    value_cols = wv.shape[1]
    col_start = head_rank * width
    gain1_part = lax.dynamic_slice_in_dim(gain1, col_start, width)
    gain2_part = lax.dynamic_slice_in_dim(gain2, col_start, width)

    def part_of(array):
        return lax.dynamic_slice_in_dim(array, col_start, width, 1)

    def halves(array):
        split = array.T.reshape(SIDE * SIDE, CORES, -1, rows)
        pick = lambda at: lax.dynamic_index_in_dim(split, at, 1, False).reshape(-1, rows)
        return pick(core), pick(1 - core)

    offsets = jnp.arange(rows, dtype=jnp.int32)
    positions = seq_rank * rows + offsets
    member = positions[:, None] >= starts[None, :]
    doc_ids = jnp.sum(member.astype(jnp.int32), axis=-1) - 1
    last_start = jnp.max(jnp.where(member, starts[None, :], 0), axis=-1)
    relative = (positions - last_start).astype(F32)
    prior_doc = jnp.sum((seq_rank * rows - 1 >= starts).astype(jnp.int32)) - 1
    half_dim = KEY_DIM // 2
    frequency = jnp.exp(-math.log(10000.0) * jnp.arange(half_dim, dtype=F32) / half_dim)
    angles = relative[:, None] * frequency[None, :]
    cosine = jnp.cos(angles)[:, None, :]
    sine = jnp.sin(angles)[:, None, :]
    head_ids = (head_rank * heads + jnp.arange(heads, dtype=jnp.int32)).astype(F32)
    log_decay = jnp.log1p(-jnp.exp2(-5.0 - head_ids))
    gap_grid = offsets[:, None] - offsets[None, :]
    keep = (gap_grid >= 0) & (doc_ids[:, None] == doc_ids[None, :])
    gap_float = jnp.where(gap_grid >= 0, gap_grid, 0).astype(F32)
    decay_grid = jnp.where(keep[None], jnp.exp(gap_float[None] * log_decay[:, None, None]), 0.0)
    step_float = offsets.astype(F32)
    arrival = jnp.exp((step_float[:, None] + 1.0) * log_decay[None, :]) * (
        doc_ids == prior_doc
    ).astype(F32)[:, None]
    departure = jnp.exp((rows - 1.0 - step_float)[:, None] * log_decay[None, :]) * (
        doc_ids == doc_ids[rows - 1]
    ).astype(F32)[:, None]
    arrival = arrival[:, :, None]
    departure = departure[:, :, None]
    segment_decay = jnp.exp(rows * log_decay)

    whole_rows = assemble(gather_parts(layer_in), head_rank).astype(F32)
    normed1, inverse1 = norm_forward(whole_rows)
    norm_low = (normed1 * gain1).astype(BF16)
    grad_full = lax.all_gather(after(cotangent, norm_low), "head", axis=1, tiled=True)
    key_rows = rotate_pairs(
        dot(norm_low, wk).reshape(rows, heads, KEY_DIM), cosine, sine, 1.0
    ).astype(BF16)
    value_rows = dot(norm_low, wv).astype(BF16).reshape(rows, heads, VALUE_DIM)
    own_state = einsum("thk,thv->hkv", key_rows.astype(F32) * departure, value_rows)
    incoming = state_scan(own_state, segment_decay, place, False)
    query_rows = rotate_pairs(
        dot(norm_low, wq).reshape(rows, heads, KEY_DIM), cosine, sine, 1.0
    ).astype(BF16)
    gate_pre = dot(norm_low, wg)
    scores = einsum("thk,shk->hts", query_rows, key_rows)
    weighted = (scores * decay_grid).astype(BF16)
    within = einsum("hts,shv->thv", weighted, value_rows)
    retained = within + arrival * einsum("thk,hkv->thv", query_rows, incoming)
    centered = retained - jnp.mean(retained, axis=-1, keepdims=True)
    group_inv = lax.rsqrt(jnp.mean(centered * centered, axis=-1, keepdims=True) + float(KEY_DIM))
    grouped = centered * group_inv
    flat_group = grouped.reshape(rows, value_cols)
    gate_sigmoid = jax.nn.sigmoid(gate_pre)
    swish = gate_pre * gate_sigmoid
    mixed = (flat_group * swish).astype(BF16)
    branch_part = scatter_cols(dot(mixed, wo).astype(BF16), head_rank).astype(BF16)
    branch = assemble(gather_parts(branch_part), head_rank).astype(F32)
    middle = whole_rows + branch
    normed2, inverse2 = norm_forward(middle)
    ffn_input = (normed2 * gain2).astype(BF16)
    hidden_pre = dot(ffn_input, w1)
    cdf = 0.5 * (1.0 + lax.erf(hidden_pre * (2.0**-0.5)))
    hidden = (hidden_pre * cdf).astype(BF16)
    pdf = jnp.exp(-0.5 * hidden_pre * hidden_pre) * ((2.0 * math.pi) ** -0.5)
    grad_hidden = dot_t(grad_full, w2)
    grad_pre = ((cdf + hidden_pre * pdf) * grad_hidden).astype(BF16)

    def norm_back(partial_grad, gain, gain_part, normed, normed_part, inverse):
        low = partial_grad.astype(BF16)
        scaled = partial_grad * gain
        sums = sum_heads(
            jnp.stack([jnp.sum(scaled, axis=-1), jnp.sum(scaled * normed, axis=-1)])
        )
        grad = scatter_cols(low, head_rank)
        gain_grad = jnp.sum(grad * normed_part, axis=0)
        back = inverse * (
            grad * gain_part
            - sums[0][:, None] / model
            - normed_part * (sums[1][:, None] / model)
        )
        return back, gain_grad

    normed2_part = part_of(normed2)
    back2, gain2_grad = norm_back(
        dot_t(grad_pre, w1), gain2, gain2_part, normed2, normed2_part, inverse2
    )
    grad_middle = cotangent.astype(F32) + back2
    grad_branch = assemble(gather_parts(grad_middle.astype(BF16)), head_rank)
    cot_halves = halves(grad_full)
    grad_w2 = weight_scatter(cot_halves, hidden, place, True)
    grad_w1 = weight_scatter(halves(ffn_input), grad_pre, place, False)
    ffn_out = dot(hidden, w2).astype(BF16)
    ffn_part = lax.psum_scatter(
        after(ffn_out, grad_branch), "head", scatter_dimension=1, tiled=True
    ).astype(F32)
    output = (part_of(middle) + ffn_part).astype(BF16)

    grad_mixed = dot_t(grad_branch, wo)
    grad_gate = (
        grad_mixed * flat_group * (gate_sigmoid * (1.0 + gate_pre * (1.0 - gate_sigmoid)))
    ).astype(BF16)
    grad_group = (grad_mixed * swish).reshape(rows, heads, VALUE_DIM)
    grad_retained = group_inv * (
        grad_group
        - jnp.mean(grad_group, axis=-1, keepdims=True)
        - grouped * jnp.mean(grad_group * grouped, axis=-1, keepdims=True)
    )
    low_grad = grad_retained.astype(BF16)
    own_back = einsum("thk,thv->hkv", query_rows, grad_retained * arrival)
    outgoing = state_scan(own_back, segment_decay, place, True)
    grad_scores = (einsum("thv,shv->hts", low_grad, value_rows) * decay_grid).astype(BF16)
    grad_query = einsum("hts,shk->thk", grad_scores, key_rows) + arrival * einsum(
        "thv,hkv->thk", low_grad, incoming
    )
    grad_qpre = rotate_pairs(grad_query, cosine, sine, -1.0).reshape(rows, -1).astype(BF16)
    grad_wo = weight_scatter(halves(grad_branch), mixed, place, True)
    norm_halves = halves(norm_low)
    grad_wg = weight_scatter(norm_halves, grad_gate, place, False)
    grad_key = einsum("hts,thk->shk", grad_scores, query_rows) + departure * einsum(
        "shv,hkv->shk", value_rows, outgoing
    )
    grad_value = einsum("hts,thv->shv", weighted, low_grad) + departure * einsum(
        "shk,hkv->shv", key_rows, outgoing
    )
    grad_kpre = rotate_pairs(grad_key, cosine, sine, -1.0).reshape(rows, -1).astype(BF16)
    grad_vpre = grad_value.reshape(rows, -1).astype(BF16)
    grad_wv = weight_scatter(norm_halves, grad_vpre, place, True)
    grad_qk = jnp.concatenate([grad_qpre, grad_kpre], axis=1)
    grad_wqk = weight_scatter(norm_halves, grad_qk, place, False)
    back_terms = (
        dot_t(grad_qpre, wq)
        + dot_t(grad_kpre, wk)
        + dot_t(grad_vpre, wv)
        + dot_t(grad_gate, wg)
    )
    back1, gain1_grad = norm_back(
        back_terms, gain1, gain1_part, normed1, part_of(normed1), inverse1
    )
    grad_x = grad_middle + back1
    gain1_total, gain2_total = lax.psum((gain1_grad, gain2_grad), "seq")
    return (
        output,
        grad_x,
        gain1_total,
        grad_wqk[:, : wq.shape[1]],
        grad_wqk[:, wq.shape[1] :],
        grad_wv,
        grad_wg,
        grad_wo.T,
        gain2_total,
        grad_w1,
        grad_w2.T,
    )


def solution(mesh):
    rows = P("seq", "head")
    return jax.shard_map(
        shards,
        mesh=mesh,
        in_specs=(
            rows,
            P(),
            P(None, "head"),
            P(None, "head"),
            P(None, "head"),
            P(None, "head"),
            P("head", None),
            P(),
            P(None, "head"),
            P("head", None),
            P(),
            rows,
        ),
        out_specs=(
            rows,
            rows,
            P("head"),
            rows,
            rows,
            rows,
            rows,
            P("head", "seq"),
            P("head"),
            rows,
            P("head", "seq"),
        ),
        check_vma=False,
    )
```

time: 1240 us -> 632 us (0.51)
  waiting for transfers between devices: 774 us -> 174 us
  starting transfers between devices: 2.03 us -> 119 us
  other arithmetic: 158 us -> 66.3 us
  blocking collectives: 106 us -> 67.7 us
  local copies, waits for them, and re-layouts: 34.7 us -> 72.7 us
  matrix products: 138 us -> 103 us
    reduce_scatter x10 -> x1, waiting for transfers between devices: 483 us -> 0.01 us  [shards(): lax.psum_scatter(after(ffn_out, grad_branch), 'head', scatter_dimension=1...]
    all_gather x5 -> x1, waiting for transfers between devices: 232 us -> 0.01 us  [shards(): lax.all_gather(after(cotangent, norm_low), 'head', axis=1, tiled=True)]
    ppermute x0 -> x88, waiting for transfers between devices: none -> 174 us  [the longest x36 59.3 us: axis_phase(): received = [lax.ppermute(block(k), 'seq', shift_of(k)) for k in (2, 1, 3)]]
    ppermute x0 -> x88, starting transfers between devices: none -> 118 us  [the longest x36 50.2 us: axis_phase(): received = [lax.ppermute(block(k), 'seq', shift_of(k)) for k in (2, 1, 3)]]
    select_n x64 -> x0, other arithmetic: 104 us -> none  [hop(): return jax.tree.map(lambda a, b: jnp.where(reached, a, b), new, before)]
    psum x1 -> x0, waiting for transfers between devices: 57.4 us -> none  [shards(): lax.psum(jnp.dot(mixed, wo, preferred_element_type=jnp.float32).astype(jn...]
    dot_general x46 -> x40, matrix products: 138 us -> 103 us  [the longest x19 59.1 us: dot(): return jnp.dot(left, right, preferred_element_type=F32)]
    all_gather x1 -> x0, blocking collectives: 21.7 us -> none  [entering(): everything = jax.tree.map(lambda part: lax.all_gather(part, axis), x)]
  transfers between devices with their start and end apart: 16 -> 90, of which waited for: 15 -> 44; matrix products, arithmetic and copies ran while one was open for 14% -> 27% of each run, Pallas kernels for 0% -> 0%
where the time goes in v1:
time: 632 us; the launch traced here: 621 us
  waiting for transfers between devices  174 us (28%)
  starting transfers between devices  119 us (19%)
  matrix products  103 us (16%)
  local copies, waits for them, and re-layouts  72.7 us (12%)
  blocking collectives  67.7 us (11%)
  other arithmetic  66.3 us (10%)
  between operations  18.5 us (3%)
    psum x1, blocking collectives, shards(): gain1_total, gain2_total = lax.psum((gain1_grad, gain2_grad), 'seq')  67.7 us
    ppermute x36, waiting for transfers between devices, axis_phase(): received = [lax.ppermute(block(k), 'seq', shift_of(k)) for k in (2, 1, 3)]  59.3 us
    dot_general x19, matrix products, dot(): return jnp.dot(left, right, preferred_element_type=F32)  59.1 us
    ppermute x9, waiting for transfers between devices, scatter_cols(): lax.ppermute(block(k), 'head', head_shift(k))  51.8 us
    ppermute x36, starting transfers between devices, axis_phase(): received = [lax.ppermute(block(k), 'seq', shift_of(k)) for k in (2, 1, 3)]  50.2 us
    ppermute x9, waiting for transfers between devices, gather_parts(): lax.ppermute(block, 'head', head_shift(k))  41 us
    dot_general x7, matrix products, dot_t(): lax.dot_general(left, right, (((1,), (1,)), ((), ())), preferred_element_...  27.9 us
    ppermute x9, starting transfers between devices, scatter_cols(): lax.ppermute(block(k), 'head', head_shift(k))  18 us
  transfers between devices with their start and end apart: 90, of which 44 were waited for; matrix products, arithmetic and copies ran while one was open for 27% of the time, Pallas kernels for 0%

profile of v1, /device:TPU:0, one launch (start us, length us, event | category | flops | bytes accessed | tf_op | source)
XLA Modules:
  0.0 620.7 jit_solution(8914495778874935361)
XLA Ops:
  26.9 7.3 %collective-permute-done.1 = bf16[512,512]{1,0:T(8,128)(2,1)} collective-permute-done((bf16[512,512]{1,0:T(8,128)(2,1)}, bf16[512,512]{1,0:T(8,128)(2,1)}, u32[]{:S(2)}, u32[]{:S(2)}) %collective-permute-start.1) | collective-permute-done | bytes 524320 | tf_op jit(solution)/shard_map/ppermute | solution.py:52
  57.0 5.3 convolution_convert_fusion.8
  106.1 7.5 %multiply_convert_fusion.6 = (bf16[512,1024]{1,0:T(8,128)(2,1)S(1)}, f32[512,1024]{1,0:T(8,128)}) fusion(f32[512,1024]{1,0:T(8,128)} %copy.110, bf16[512,2048]{1,0:T(8,128)(2,1)} %copy-done.37, bf16[2048,1024]{1,0:T(8,128)(2,1)} %param.17), kind=kOutput, calls=%fused_computation.46 | convolution fusion | flops 2150629376 | bytes 11534336 | tf_op jit(solution)/shard_map/dot_general | solution.py:36
  118.5 4.1 collective-permute-start.14
  127.6 8.0 %collective-permute-done.14 = bf16[512,512]{1,0:T(8,128)(2,1)} collective-permute-done((bf16[512,512]{1,0:T(8,128)(2,1)}, bf16[512,512]{1,0:T(8,128)(2,1)}, u32[]{:S(2)}, u32[]{:S(2)}) %collective-permute-start.14) | collective-permute-done | bytes 524320 | tf_op jit(solution)/shard_map/ppermute | solution.py:71
  135.7 10.7 %collective-permute-done.15 = bf16[512,512]{1,0:T(8,128)(2,1)} collective-permute-done((bf16[512,512]{1,0:T(8,128)(2,1)}, bf16[512,512]{1,0:T(8,128)(2,1)}, u32[]{:S(2)}, u32[]{:S(2)}) %collective-permute-start.15) | collective-permute-done | bytes 524320 | tf_op jit(solution)/shard_map/ppermute | solution.py:71
  174.4 11.2 %collective-permute-done.19 = bf16[512,512]{1,0:T(8,128)(2,1)} collective-permute-done((bf16[512,512]{1,0:T(8,128)(2,1)}, bf16[512,512]{1,0:T(8,128)(2,1)}, u32[]{:S(2)}, u32[]{:S(2)}) %collective-permute-start.19) | collective-permute-done | bytes 524320 | tf_op jit(solution)/shard_map/ppermute | solution.py:52
  187.5 4.8 convert_add_fusion
  195.5 5.9 fusion.49
  201.4 4.1 copy.138
  208.8 6.2 multiply_convert_fusion.5
  219.8 6.5 %fusion.8 = bf16[512,1024]{1,0:T(8,128)(2,1)S(1)} fusion(f32[512,1024]{1,0:T(8,128)} %get-tuple-element.152, bf16[512,2048]{0,1:T(8,128)(2,1)} %all-gather.2.cloned.1.call-done, bf16[1024,2048]{1,0:T(8,128)(2,1)} %param.21), kind=kOutput, calls=%fused_computation.29 | convolution fusion | flops 2152726528 | bytes 9437184 | tf_op jit(solution)/shard_map/dot_general | solution.py:40
  243.0 8.5 %collective-permute-done.20 = bf16[512,512]{1,0:T(8,128)(2,1)S(1)} collective-permute-done((bf16[512,512]{1,0:T(8,128)(2,1)S(1)}, bf16[512,512]{1,0:T(8,128)(2,1)S(1)}, u32[]{:S(2)}, u32[]{:S(2)}) %collective-permute-start.20) | collective-permute-done | bytes 524320 | tf_op jit(solution)/shard_map/ppermute | solution.py:71
  251.4 6.0 collective-permute-done.21
  266.6 18.7 %collective-permute-done.26 = bf16[512,512]{1,0:T(8,128)(2,1)S(1)} collective-permute-done((bf16[512,512]{1,0:T(8,128)(2,1)S(1)}, bf16[512,512]{1,0:T(8,128)(2,1)S(1)}, u32[]{:S(2)}, u32[]{:S(2)}) %collective-permute-start.26) | collective-permute-done | bytes 524320 | tf_op jit(solution)/shard_map/ppermute | solution.py:52
  285.6 4.7 fusion.71
  314.2 4.4 fusion.142
  389.6 7.8 %collective-permute-done.40 = bf16[512,512]{1,0:T(8,128)(2,1)S(1)} collective-permute-done((bf16[512,512]{1,0:T(8,128)(2,1)S(1)}, bf16[512,512]{1,0:T(8,128)(2,1)S(1)}, u32[]{:S(2)}, u32[]{:S(2)}) %collective-permute-start.40) | collective-permute-done | bytes 524320 | tf_op jit(solution)/shard_map/ppermute | solution.py:71
  397.4 10.7 %collective-permute-done.41 = bf16[512,512]{1,0:T(8,128)(2,1)S(1)} collective-permute-done((bf16[512,512]{1,0:T(8,128)(2,1)S(1)}, bf16[512,512]{1,0:T(8,128)(2,1)S(1)}, u32[]{:S(2)}, u32[]{:S(2)}) %collective-permute-start.41) | collective-permute-done | bytes 524320 | tf_op jit(solution)/shard_map/ppermute | solution.py:71
  416.9 6.9 %collective-permute-done.83 = bf16[4,64,1024]{2,1,0:T(8,128)(2,1)S(1)} collective-permute-done((bf16[4,64,1024]{2,1,0:T(8,128)(2,1)S(1)}, bf16[4,64,1024]{2,1,0:T(8,128)(2,1)S(1)}, u32[]{:S(2)}, u32[]{:S(2)}) %collective-permute-start.83) | collective-permute-done | bytes 524320 | tf_op jit(solution)/shard_map/ppermute | solution.py:89
  428.6 67.7 %all-reduce = (f32[512]{0:T(512)}, f32[512]{0:T(512)}) all-reduce(f32[512]{0:T(512)S(1)} %get-tuple-element.40, f32[512]{0:T(512)S(1)} %copy-done.76), channel_id=1, replica_groups=mesh['seq'=32,'head'=4] {'seq'}, use_global_device_ids=true, to_apply=%region_19.20 | all-reduce | flops 1024 | bytes 8192 | tf_op jit(solution)/shard_map/psum | solution.py:356
  523.4 7.8 %collective-permute-done.68 = bf16[4,64,1024]{2,1,0:T(8,128)(2,1)S(1)} collective-permute-done((bf16[4,64,1024]{2,1,0:T(8,128)(2,1)S(1)}, bf16[4,64,1024]{2,1,0:T(8,128)(2,1)S(1)}, u32[]{:S(2)}, u32[]{:S(2)}) %collective-permute-start.68) | collective-permute-done | bytes 524320 | tf_op jit(solution)/shard_map/ppermute | solution.py:89
  532.3 9.4 %collective-permute-done.69 = bf16[4,64,1024]{2,1,0:T(8,128)(2,1)S(1)} collective-permute-done((bf16[4,64,1024]{2,1,0:T(8,128)(2,1)S(1)}, bf16[4,64,1024]{2,1,0:T(8,128)(2,1)S(1)}, u32[]{:S(2)}, u32[]{:S(2)}) %collective-permute-start.69) | collective-permute-done | bytes 524320 | tf_op jit(solution)/shard_map/ppermute | solution.py:89
  546.3 11.4 %collective-permute-done.62 = bf16[4,64,1024]{2,1,0:T(8,128)(2,1)S(1)} collective-permute-done((bf16[4,64,1024]{2,1,0:T(8,128)(2,1)S(1)}, bf16[4,64,1024]{2,1,0:T(8,128)(2,1)S(1)}, u32[]{:S(2)}, u32[]{:S(2)}) %collective-permute-start.62) | collective-permute-done | bytes 524320 | tf_op jit(solution)/shard_map/ppermute | solution.py:89
  (555 shorter events, 356.6 us)
Async XLA Ops:
  7.2 212.6 %all-gather.2.cloned.1.call-start = ((), (), s32[]{:S(2)}) async-start(), calls=%async_computation.1 | async-start | bytes 2621440 | tf_op jit(solution)/shard_map/all_gather | solution.py:250
  9.3 25.0 %collective-permute-start.1 = (bf16[512,512]{1,0:T(8,128)(2,1)}, bf16[512,512]{1,0:T(8,128)(2,1)}, u32[]{:S(2)}, u32[]{:S(2)}) collective-permute-start(bf16[512,512]{1,0:T(8,128)(2,1)} %param.12), channel_id=1, source_target_pairs={{0,3},{1,0},{2,1},{3,2},{4,7},{5,4},{6,5},{7,6},{8,11},{9,8},{10,9... | collective-permute-start | bytes 1572872 | tf_op jit(solution)/shard_map/ppermute | solution.py:52
  11.5 24.7 %collective-permute-start.2 = (bf16[512,512]{1,0:T(8,128)(2,1)}, bf16[512,512]{1,0:T(8,128)(2,1)}, u32[]{:S(2)}, u32[]{:S(2)}) collective-permute-start(bf16[512,512]{1,0:T(8,128)(2,1)} %param.12), channel_id=1, source_target_pairs={{0,2},{1,3},{2,0},{3,1},{4,6},{5,7},{6,4},{7,5},{8,10},{9,11},{10,... | collective-permute-start | bytes 1572872 | tf_op jit(solution)/shard_map/ppermute | solution.py:52
  122.6 23.8 %collective-permute-start.15 = (bf16[512,512]{1,0:T(8,128)(2,1)}, bf16[512,512]{1,0:T(8,128)(2,1)}, u32[]{:S(2)}, u32[]{:S(2)}) collective-permute-start(bf16[512,512]{1,0:T(8,128)(2,1)} %get-tuple-element.83), channel_id=1, source_target_pairs={{0,1},{1,2},{2,3},{3,0},{4,5},{5,6},{6,7},{7,4},{8,9},{9,10},{10,1... | collective-permute-start | bytes 1572872 | tf_op jit(solution)/shard_map/ppermute | solution.py:71
  123.0 23.5 %collective-permute-start.16 = (bf16[512,512]{1,0:T(8,128)(2,1)S(1)}, bf16[512,512]{1,0:T(8,128)(2,1)}, u32[]{:S(2)}, u32[]{:S(2)}) collective-permute-start(bf16[512,512]{1,0:T(8,128)(2,1)S(1)} %get-tuple-element.82), channel_id=1, source_target_pairs={{0,3},{1,0},{2,1},{3,2},{4,7},{5,4},{6,5},{7,6},{8,11},{9,8},{10,9... | collective-permute-start | bytes 1572872 | tf_op jit(solution)/shard_map/ppermute | solution.py:71
  154.2 31.4 %collective-permute-start.19 = (bf16[512,512]{1,0:T(8,128)(2,1)}, bf16[512,512]{1,0:T(8,128)(2,1)}, u32[]{:S(2)}, u32[]{:S(2)}) collective-permute-start(bf16[512,512]{1,0:T(8,128)(2,1)} %get-tuple-element.35), channel_id=1, source_target_pairs={{0,2},{1,3},{2,0},{3,1},{4,6},{5,7},{6,4},{7,5},{8,10},{9,11},{10,... | collective-permute-start | bytes 1572872 | tf_op jit(solution)/shard_map/ppermute | solution.py:52
  159.7 451.4 %reduce-scatter.2.cloned.1.call-start = ((), (), s32[]{:S(2)}) async-start(), calls=%async_computation.2 | async-start | bytes 2621440 | tf_op jit(solution)/shard_map/reduce_scatter | solution.py:309
  242.9 140.4 %collective-permute-start.81 = (bf16[1024,1024]{1,0:T(8,128)(2,1)}, bf16[1024,1024]{1,0:T(8,128)(2,1)}, u32[]{:S(2)}, u32[]{:S(2)}) collective-permute-start(bf16[1024,1024]{1,0:T(8,128)(2,1)} %convolution_convert_fusion.2), channel_id=1, source_target_pairs={{0,4},{4,0},{8,12},{12,8},{16,20},{20,16},{24,28},{28,24},{32,36},... | collective-permute-start | bytes 6291464 | tf_op jit(solution)/shard_map/ppermute | solution.py:101
  259.2 26.1 %collective-permute-start.26 = (bf16[512,512]{1,0:T(8,128)(2,1)S(1)}, bf16[512,512]{1,0:T(8,128)(2,1)S(1)}, u32[]{:S(2)}, u32[]{:S(2)}) collective-permute-start(bf16[512,512]{1,0:T(8,128)(2,1)S(1)} %get-tuple-element.32), channel_id=1, source_target_pairs={{0,1},{1,2},{2,3},{3,0},{4,5},{5,6},{6,7},{7,4},{8,9},{9,10},{10,1... | collective-permute-start | bytes 1572872 | tf_op jit(solution)/shard_map/ppermute | solution.py:52
  260.3 25.1 %collective-permute-start.27 = (bf16[512,512]{1,0:T(8,128)(2,1)S(1)}, bf16[512,512]{1,0:T(8,128)(2,1)S(1)}, u32[]{:S(2)}, u32[]{:S(2)}) collective-permute-start(bf16[512,512]{1,0:T(8,128)(2,1)S(1)} %get-tuple-element.32), channel_id=1, source_target_pairs={{0,3},{1,0},{2,1},{3,2},{4,7},{5,4},{6,5},{7,6},{8,11},{9,8},{10,9... | collective-permute-start | bytes 1572872 | tf_op jit(solution)/shard_map/ppermute | solution.py:52
  262.5 23.0 %collective-permute-start.28 = (bf16[512,512]{1,0:T(8,128)(2,1)S(1)}, bf16[512,512]{1,0:T(8,128)(2,1)S(1)}, u32[]{:S(2)}, u32[]{:S(2)}) collective-permute-start(bf16[512,512]{1,0:T(8,128)(2,1)S(1)} %get-tuple-element.32), channel_id=1, source_target_pairs={{0,2},{1,3},{2,0},{3,1},{4,6},{5,7},{6,4},{7,5},{8,10},{9,11},{10,... | collective-permute-start | bytes 1572872 | tf_op jit(solution)/shard_map/ppermute | solution.py:52
  265.6 123.9 %collective-permute-start.74 = (bf16[1024,1024]{1,0:T(8,128)(2,1)}, bf16[1024,1024]{1,0:T(8,128)(2,1)}, u32[]{:S(2)}, u32[]{:S(2)}) collective-permute-start(bf16[1024,1024]{1,0:T(8,128)(2,1)} %convolution_convert_fusion.3), channel_id=1, source_target_pairs={{0,4},{4,0},{8,12},{12,8},{16,20},{20,16},{24,28},{28,24},{32,36},... | collective-permute-start | bytes 6291464 | tf_op jit(solution)/shard_map/ppermute | solution.py:101
  380.9 125.9 %collective-permute-start.67 = (bf16[1024,1024]{1,0:T(8,128)(2,1)}, bf16[1024,1024]{1,0:T(8,128)(2,1)}, u32[]{:S(2)}, u32[]{:S(2)}) collective-permute-start(bf16[1024,1024]{1,0:T(8,128)(2,1)} %convolution_convert_fusion.4), channel_id=1, source_target_pairs={{0,4},{4,0},{8,12},{12,8},{16,20},{20,16},{24,28},{28,24},{32,36},... | collective-permute-start | bytes 6291464 | tf_op jit(solution)/shard_map/ppermute | solution.py:101
  383.0 25.2 %collective-permute-start.41 = (bf16[512,512]{1,0:T(8,128)(2,1)S(1)}, bf16[512,512]{1,0:T(8,128)(2,1)S(1)}, u32[]{:S(2)}, u32[]{:S(2)}) collective-permute-start(bf16[512,512]{1,0:T(8,128)(2,1)S(1)} %get-tuple-element.77), channel_id=1, source_target_pairs={{0,1},{1,2},{2,3},{3,0},{4,5},{5,6},{6,7},{7,4},{8,9},{9,10},{10,1... | collective-permute-start | bytes 1572872 | tf_op jit(solution)/shard_map/ppermute | solution.py:71
  383.3 24.8 %collective-permute-start.42 = (bf16[512,512]{1,0:T(8,128)(2,1)S(1)}, bf16[512,512]{1,0:T(8,128)(2,1)S(1)}, u32[]{:S(2)}, u32[]{:S(2)}) collective-permute-start(bf16[512,512]{1,0:T(8,128)(2,1)S(1)} %get-tuple-element.76), channel_id=1, source_target_pairs={{0,3},{1,0},{2,1},{3,2},{4,7},{5,4},{6,5},{7,6},{8,11},{9,8},{10,9... | collective-permute-start | bytes 1572872 | tf_op jit(solution)/shard_map/ppermute | solution.py:71
  389.5 127.4 %collective-permute-start.60 = (bf16[1024,1024]{1,0:T(8,128)(2,1)}, bf16[1024,1024]{1,0:T(8,128)(2,1)}, u32[]{:S(2)}, u32[]{:S(2)}) collective-permute-start(bf16[1024,1024]{1,0:T(8,128)(2,1)} %convolution_convert_fusion.5), channel_id=1, source_target_pairs={{0,4},{4,0},{8,12},{12,8},{16,20},{20,16},{24,28},{28,24},{32,36},... | collective-permute-start | bytes 6291464 | tf_op jit(solution)/shard_map/ppermute | solution.py:101
  415.5 82.8 %collective-permute-start.75 = (bf16[4,64,1024]{2,1,0:T(8,128)(2,1)}, bf16[4,64,1024]{2,1,0:T(8,128)(2,1)}, u32[]{:S(2)}, u32[]{:S(2)}) collective-permute-start(bf16[4,64,1024]{2,1,0:T(8,128)(2,1)} %get-tuple-element.54), channel_id=1, source_target_pairs={{0,16},{4,20},{8,24},{12,28},{16,0},{20,4},{24,8},{28,12},{32,48},... | collective-permute-start | bytes 1572872 | tf_op jit(solution)/shard_map/ppermute | solution.py:89
  423.8 74.6 %collective-permute-start.76 = (bf16[4,64,1024]{2,1,0:T(8,128)(2,1)}, bf16[4,64,1024]{2,1,0:T(8,128)(2,1)}, u32[]{:S(2)}, u32[]{:S(2)}) collective-permute-start(bf16[4,64,1024]{2,1,0:T(8,128)(2,1)} %get-tuple-element.56), channel_id=1, source_target_pairs={{0,8},{4,12},{8,16},{12,20},{16,24},{20,28},{24,0},{28,4},{32,40},... | collective-permute-start | bytes 1572872 | tf_op jit(solution)/shard_map/ppermute | solution.py:89
  424.6 73.9 %collective-permute-start.77 = (bf16[4,64,1024]{2,1,0:T(8,128)(2,1)}, bf16[4,64,1024]{2,1,0:T(8,128)(2,1)}, u32[]{:S(2)}, u32[]{:S(2)}) collective-permute-start(bf16[4,64,1024]{2,1,0:T(8,128)(2,1)} %get-tuple-element.55), channel_id=1, source_target_pairs={{0,24},{4,28},{8,0},{12,4},{16,8},{20,12},{24,16},{28,20},{32,56},... | collective-permute-start | bytes 1572872 | tf_op jit(solution)/shard_map/ppermute | solution.py:89
  504.9 62.1 %collective-permute-start.46 = (bf16[1024,1024]{1,0:T(8,128)(2,1)S(1)}, bf16[1024,1024]{1,0:T(8,128)(2,1)S(1)}, u32[]{:S(2)}, u32[]{:S(2)}) collective-permute-start(bf16[1024,1024]{1,0:T(8,128)(2,1)S(1)} %copy-done.85), channel_id=1, source_target_pairs={{0,4},{4,0},{8,12},{12,8},{16,20},{20,16},{24,28},{28,24},{32,36},... | collective-permute-start | bytes 6291464 | tf_op jit(solution)/shard_map/ppermute | solution.py:101
  514.6 57.3 %collective-permute-start.53 = (bf16[1024,1024]{1,0:T(8,128)(2,1)S(1)}, bf16[1024,1024]{1,0:T(8,128)(2,1)S(1)}, u32[]{:S(2)}, u32[]{:S(2)}) collective-permute-start(bf16[1024,1024]{1,0:T(8,128)(2,1)S(1)} %copy-done.84), channel_id=1, source_target_pairs={{0,4},{4,0},{8,12},{12,8},{16,20},{20,16},{24,28},{28,24},{32,36},... | collective-permute-start | bytes 6291464 | tf_op jit(solution)/shard_map/ppermute | solution.py:101
  516.9 24.8 %collective-permute-start.69 = (bf16[4,64,1024]{2,1,0:T(8,128)(2,1)S(1)}, bf16[4,64,1024]{2,1,0:T(8,128)(2,1)S(1)}, u32[]{:S(2)}, u32[]{:S(2)}) collective-permute-start(bf16[4,64,1024]{2,1,0:T(8,128)(2,1)S(1)} %get-tuple-element.61), channel_id=1, source_target_pairs={{0,32},{4,36},{8,40},{12,44},{16,48},{20,52},{24,56},{28,60},{32,6... | collective-permute-start | bytes 1572872 | tf_op jit(solution)/shard_map/ppermute | solution.py:89
  516.9 25.3 %collective-permute-start.70 = (bf16[4,64,1024]{2,1,0:T(8,128)(2,1)S(1)}, bf16[4,64,1024]{2,1,0:T(8,128)(2,1)S(1)}, u32[]{:S(2)}, u32[]{:S(2)}) collective-permute-start(bf16[4,64,1024]{2,1,0:T(8,128)(2,1)S(1)} %get-tuple-element.60), channel_id=1, source_target_pairs={{0,96},{4,100},{8,104},{12,108},{16,112},{20,116},{24,120},{28,124... | collective-permute-start | bytes 1572872 | tf_op jit(solution)/shard_map/ppermute | solution.py:89
  569.2 21.3 %collective-permute-start.48 = (bf16[4,64,1024]{2,1,0:T(8,128)(2,1)S(1)}, bf16[4,64,1024]{2,1,0:T(8,128)(2,1)S(1)}, u32[]{:S(2)}, u32[]{:S(2)}) collective-permute-start(bf16[4,64,1024]{2,1,0:T(8,128)(2,1)S(1)} %get-tuple-element.72), channel_id=1, source_target_pairs={{0,8},{4,12},{8,16},{12,20},{16,24},{20,28},{24,0},{28,4},{32,40},... | collective-permute-start | bytes 1572872 | tf_op jit(solution)/shard_map/ppermute | solution.py:89
  (166 other events, 1943.7 us)
Sparse Core Ops, SparseCore 0:
  159.9 35.6 all-gather.1
  328.0 28.5 reduce-scatter.1

commit v2 on v1

v2 whole, which is shorter than its diff:
```python
import math

import jax
import jax.numpy as jnp
from jax import lax
from jax.experimental import pallas as pl
from jax.experimental.pallas import tpu as pltpu
from jax.sharding import PartitionSpec as P

KEY = 256
VAL = 512
SIDE = 4
CORES = 2
HEADS = 2
ROWS = 512
HALF = 256
PART = 512
MODEL = 2048
EXTRA = 16
EPSILON = 1e-05
F32 = jnp.float32
BF16 = jnp.bfloat16
VMEM_BYTES = 48 * 1024 * 1024
ORDER = (2, 1, 3, 0)


def head_shift(step):
    return [(h, (h + step) % SIDE) for h in range(SIDE)]


def seq_index(x, y, core):
    return (x * SIDE + y) * CORES + core


def seq_shift(dx, dy, swap=0):
    return [
        (seq_index(x, y, core), seq_index((x + dx) % SIDE, (y + dy) % SIDE, core ^ swap))
        for x in range(SIDE)
        for y in range(SIDE)
        for core in range(CORES)
    ]


SWAP = seq_shift(0, 0, 1)


def up(block):
    return lax.ppermute(block, "head", head_shift(1))


def down(block):
    return lax.ppermute(block, "head", head_shift(SIDE - 1))


def add_low(a, b):
    return (a.astype(F32) + b.astype(F32)).astype(BF16)


def ring_gather(a, b):
    r1, l1 = up(a), down(b)
    r2, l2 = up(b), down(a)
    r3, l3 = up(r1), down(l1)
    return [a, b, r1, r2, r3, l3, l2, l1]


def ring_scatter(p2a, p2b, p1a, p1b, pma, pmb):
    t1, t2 = up(p2a), down(p2b)
    rb, la = up(p1b), down(pma)
    ra, lb = up(add_low(p1a, t1)), down(add_low(pmb, t2))
    return [ra, rb, la, lb]


def whole(shape):
    return pl.BlockSpec(shape, lambda *_: (0,) * len(shape))


def call(name, body, grid, scalars, ins, outs, tokens=(), scratch=(), flops=0):
    arrays = [item[0] for item in ins]
    in_specs = [whole(i[0].shape) if len(i) == 1 else pl.BlockSpec(i[1], i[2]) for i in ins]
    out_specs = [whole(o[0]) if len(o) == 2 else pl.BlockSpec(o[2], o[3]) for o in outs]
    out_shape = [jax.ShapeDtypeStruct(o[0], o[1]) for o in outs]
    n_in, n_tok, n_sc = len(arrays), len(tokens), len(scalars)
    in_specs += [pl.BlockSpec(memory_space=pl.ANY)] * n_tok

    def run(*refs):
        body(*refs[: n_sc + n_in], *refs[n_sc + n_in + n_tok :])

    moved = sum(a.size * a.dtype.itemsize for a in arrays) + sum(
        math.prod(o[0]) * jnp.dtype(o[1]).itemsize for o in outs
    )
    return pl.pallas_call(
        run,
        name=name,
        grid_spec=pltpu.PrefetchScalarGridSpec(
            num_scalar_prefetch=n_sc,
            grid=grid,
            in_specs=in_specs,
            out_specs=out_specs,
            scratch_shapes=list(scratch),
        ),
        out_shape=out_shape,
        compiler_params=pltpu.CompilerParams(
            dimension_semantics=("arbitrary",) * len(grid), vmem_limit_bytes=VMEM_BYTES
        ),
        cost_estimate=pl.CostEstimate(flops=flops, bytes_accessed=moved, transcendentals=0),
    )(*scalars, *arrays, *tokens)


def dot(left, right):
    return jnp.dot(left, right, preferred_element_type=F32)


def dot_t(left, right):
    return lax.dot_general(left, right, (((1,), (1,)), ((), ())), preferred_element_type=F32)


def t_dot(left, right):
    return lax.dot_general(left, right, (((0,), (0,)), ((), ())), preferred_element_type=F32)


def rotate(rows, cosine, sine):
    half = rows.shape[-1] // 2
    first, second = rows[:, :half], rows[:, half:]
    return jnp.concatenate([first * cosine - second * sine, second * cosine + first * sine], axis=1)


def head_col(info, k):
    return pl.multiple_of(lax.rem(info[0] + SIDE - k, SIDE) * PART, PART)


CHUNK = 32


def norm_rows(info, load, gain, low, mean_ref, inv_ref, own=None):
    for half in range(2):

        def step(i, _):
            at = pl.multiple_of(i * CHUNK, CHUNK)
            out = pl.ds(pl.multiple_of(half * HALF + i * CHUNK, CHUNK), CHUNK)
            parts = [load(k, half, at) for k in range(SIDE)]
            if own is not None:
                own[out, :] = parts[0]
            mean = sum(jnp.sum(p, axis=1, keepdims=True) for p in parts) / MODEL
            parts = [p - mean for p in parts]
            var = sum(jnp.sum(p * p, axis=1, keepdims=True) for p in parts) / MODEL
            inv = lax.rsqrt(var + EPSILON)
            mean_ref[out, :] = mean
            inv_ref[out, :] = inv
            for k in range(SIDE):
                cols = pl.ds(head_col(info, k), PART)
                low[out, cols] = (parts[k] * inv * gain[:, cols]).astype(BF16)
            return 0

        lax.fori_loop(0, HALF // CHUNK, step, 0)


def norm1(info, parts, gain, cotangent):
    def body(info, *refs):
        x = refs[:8]
        gain, cot, low, mean, inv, cot_out = refs[8:]
        cot_out[...] = cot[...]
        norm_rows(
            info,
            lambda k, half, at: x[2 * k + half][pl.ds(at, CHUNK), :].astype(F32),
            gain,
            low,
            mean,
            inv,
        )

    return call(
        "norm1",
        body,
        (1,),
        [info],
        [(p,) for p in parts] + [(gain,), (cotangent,)],
        [
            ((ROWS, MODEL), BF16),
            ((ROWS, 1), F32),
            ((ROWS, 1), F32),
            ((ROWS, PART), BF16),
        ],
    )


def key_value(info, low, wk, wv, cosine, sine, departure):
    def body(info, low, wk, wv, cosine, sine, departure, key, value, own, give):
        head = pl.program_id(0)
        k = rotate(dot(low[...], wk[...]), cosine[...], sine[...]).astype(BF16)
        key[...] = k
        v = dot(low[...], wv[...]).astype(BF16)
        value[...] = v
        state = t_dot((k.astype(F32) * departure[0]).astype(BF16), v)

        @pl.when(head == info[1])
        def _():
            own[...] = state

        @pl.when(head != info[1])
        def _():
            give[...] = state.astype(BF16)

    by_head = lambda h, *_: (0, h)
    return call(
        "key_value",
        body,
        (HEADS,),
        [info],
        [
            (low,),
            (wk, (MODEL, KEY), by_head),
            (wv, (MODEL, VAL), by_head),
            (cosine,),
            (sine,),
            (departure, (1, ROWS, 1), lambda h, *_: (h, 0, 0)),
        ],
        [
            ((ROWS, HEADS * KEY), BF16, (ROWS, KEY), by_head),
            ((ROWS, HEADS * VAL), BF16, (ROWS, VAL), by_head),
            ((KEY, VAL), F32),
            ((KEY, VAL), BF16),
        ],
        flops=2 * ROWS * MODEL * 1536,
    )


def query_part(low, wq, key, value, decay, cosine, sine, tokens):
    def body(low, wq, key, value, decay, cosine, sine, query, weighted, within):
        q = rotate(dot(low[...], wq[...]), cosine[...], sine[...]).astype(BF16)
        query[...] = q
        w = (dot_t(q, key[...]) * decay[0]).astype(BF16)
        weighted[0] = w
        within[...] = dot(w, value[...])

    by_head = lambda h, *_: (0, h)
    cube = lambda h, *_: (h, 0, 0)
    return call(
        "query_part",
        body,
        (HEADS,),
        [],
        [
            (low,),
            (wq, (MODEL, KEY), by_head),
            (key, (ROWS, KEY), by_head),
            (value, (ROWS, VAL), by_head),
            (decay, (1, ROWS, ROWS), cube),
            (cosine,),
            (sine,),
        ],
        [
            ((ROWS, HEADS * KEY), BF16, (ROWS, KEY), by_head),
            ((HEADS, ROWS, ROWS), BF16, (1, ROWS, ROWS), cube),
            ((ROWS, HEADS * VAL), F32, (ROWS, VAL), by_head),
        ],
        tokens,
        flops=2 * ROWS * MODEL * 512 + 4 * ROWS * ROWS * 768,
    )


def matmul_cols(name, left, right, out_type, tokens=(), block=512):
    def body(left, right, out):
        out[...] = dot(left[...], right[...]).astype(out_type)

    depth, cols = right.shape
    by_col = lambda i, *_: (0, i)
    return call(
        name,
        body,
        (cols // block,),
        [],
        [(left,), (right, (depth, block), by_col)],
        [((left.shape[0], cols), out_type, (left.shape[0], block), by_col)],
        tokens,
        flops=2 * left.shape[0] * depth * cols,
    )[0]


def matmul_rows(name, left, right, out_type, tokens=(), block=256):
    def body(left, right, out):
        out[...] = dot_t(left[...], right[...]).astype(out_type)

    cols, depth = right.shape
    return call(
        name,
        body,
        (cols // block,),
        [],
        [(left,), (right, (block, depth), lambda i, *_: (i, 0))],
        [((left.shape[0], cols), out_type, (left.shape[0], block), lambda i, *_: (0, i))],
        tokens,
        flops=2 * left.shape[0] * depth * cols,
    )[0]


def block_outs(extra):
    tall = HALF + extra
    return [
        ((tall, PART), BF16),
        ((HALF, PART), BF16),
        ((tall, PART), BF16),
        ((HALF, PART), BF16),
        ((tall, PART), BF16),
        ((HALF, PART), BF16),
        ((ROWS, PART), F32),
    ]


def put_block(step, block, outs):
    for k in range(SIDE - 1):

        @pl.when(step == k)
        def _():
            outs[2 * k][:HALF, :] = block[:HALF].astype(BF16)
            outs[2 * k + 1][...] = block[HALF:].astype(BF16)

    @pl.when(step == SIDE - 1)
    def _():
        outs[6][...] = block


def pick(mine, sibling, info, head):
    return jnp.where(info[1] == head, mine[...], sibling[...])


def mix(info, within, gate, query, mine, sibling, arrival, wo):
    def body(info, within, gate, query, mine, sibling, arrival, wo, mixed, grouped, ginv, *outs):
        step = pl.program_id(0)

        @pl.when(step == 0)
        def _():
            for head in range(HEADS):
                cols = slice(head * VAL, (head + 1) * VAL)
                state = pick(mine, sibling, info, head)
                for half in range(2):
                    rows = slice(half * HALF, (half + 1) * HALF)
                    cross = dot(query[rows, head * KEY : (head + 1) * KEY], state)
                    kept = within[rows, cols] + arrival[head, rows] * cross
                    kept = kept - jnp.mean(kept, axis=1, keepdims=True)
                    inv = lax.rsqrt(jnp.mean(kept * kept, axis=1, keepdims=True) + float(KEY))
                    group = kept * inv
                    g = gate[rows, cols]
                    ginv[head, rows] = inv
                    grouped[rows, cols] = group.astype(BF16)
                    mixed[rows, cols] = (group * (g / (1.0 + jnp.exp(-g)))).astype(BF16)

        put_block(step, dot(mixed[...], wo[...]), outs)

    cols = HEADS * VAL
    return call(
        "mix",
        body,
        (SIDE,),
        [info],
        [
            (within,),
            (gate,),
            (query,),
            (mine,),
            (sibling,),
            (arrival,),
            (wo, (cols, PART), lambda i, info: (0, info[2 + i])),
        ],
        [((ROWS, cols), BF16), ((ROWS, cols), BF16), ((HEADS, ROWS, 1), F32)] + block_outs(0),
        flops=2 * ROWS * MODEL * cols,
    )


def sum_branch(p0, pieces):
    def body(p0, ra, rb, la, lb, a, b):
        a[...] = (p0[:HALF] + ra[...].astype(F32) + la[...].astype(F32)).astype(BF16)
        b[...] = (p0[HALF:] + rb[...].astype(F32) + lb[...].astype(F32)).astype(BF16)

    return call(
        "sum_branch",
        body,
        (1,),
        [],
        [(p0,)] + [(p,) for p in pieces],
        [((HALF, PART), BF16), ((HALF, PART), BF16)],
    )


def feed_up(info, x_parts, b_parts, gain, w1, grad_hidden, tokens):
    block = 256

    def body(info, *refs):
        x, b = refs[:8], refs[8:16]
        gain, w1, grad_hidden, ffn_in, mean, inv, own, hidden, grad_pre = refs[16:]

        @pl.when(pl.program_id(0) == 0)
        def _():
            def load(k, half, at):
                rows = pl.ds(at, CHUNK)
                return x[2 * k + half][rows, :].astype(F32) + b[2 * k + half][rows, :].astype(F32)

            norm_rows(info, load, gain, ffn_in, mean, inv, own)

        pre = dot(ffn_in[...], w1[...])
        cdf = 0.5 * (1.0 + lax.erf(pre * (2.0**-0.5)))
        hidden[...] = (pre * cdf).astype(BF16)
        pdf = jnp.exp(-0.5 * pre * pre) * ((2.0 * math.pi) ** -0.5)
        grad_pre[...] = ((cdf + pre * pdf) * grad_hidden[...].astype(F32)).astype(BF16)

    by_col = lambda i, *_: (0, i)
    cols = w1.shape[1]
    tall = ((ROWS, cols), BF16, (ROWS, block), by_col)
    return call(
        "feed_up",
        body,
        (cols // block,),
        [info],
        [(p,) for p in x_parts]
        + [(p,) for p in b_parts]
        + [
            (gain,),
            (w1, (MODEL, block), by_col),
            (grad_hidden, (ROWS, block), by_col),
        ],
        [
            ((ROWS, MODEL), BF16),
            ((ROWS, 1), F32),
            ((ROWS, 1), F32),
            ((ROWS, PART), F32),
            tall,
            tall,
        ],
        tokens,
        flops=2 * ROWS * MODEL * cols,
    )


def back_blocks(name, info, pairs, base, gain, low, tokens=()):
    n = len(pairs)

    def body(info, *refs):
        grads, weights = refs[:n], refs[n : 2 * n]
        rest = refs[2 * n :]
        if base is not None:
            base_ref, rest = rest[0], rest[1:]
        gain, low = rest[:2]
        outs, sums, acc = rest[2:9], rest[9], rest[10]
        step = pl.program_id(0)
        total = dot_t(grads[0][...], weights[0][...])
        for g, w in zip(grads[1:], weights[1:]):
            total = total + dot_t(g[...], w[...])
        if base is not None:
            total = total + base_ref[...]
        put_block(step, total, outs)
        first = jnp.sum(total * gain[...], axis=1, keepdims=True) / MODEL
        second = jnp.sum(total * low[...].astype(F32), axis=1, keepdims=True) / MODEL
        lane = lax.broadcasted_iota(jnp.int32, (ROWS, 128), 1)
        both = jnp.where(lane == 0, first, jnp.where(lane == 1, second, 0.0))

        @pl.when(step == 0)
        def _():
            acc[...] = both

        @pl.when(step > 0)
        def _():
            acc[...] = acc[...] + both

        @pl.when(step == SIDE - 1)
        def _():
            turned = acc[...].T[:EXTRA]
            sums[...] = turned
            for k in range(SIDE - 1):
                outs[2 * k][HALF:, :] = turned.astype(BF16)

    by_row = lambda i, info: (info[2 + i], 0)
    by_col = lambda i, info: (0, info[2 + i])
    return call(
        name,
        body,
        (SIDE,),
        [info],
        [(g,) for g, _ in pairs]
        + [(w, (PART, w.shape[1]), by_row) for _, w in pairs]
        + ([(base, (ROWS, PART), by_col)] if base is not None else [])
        + [(gain, (1, PART), by_col), (low, (ROWS, PART), by_col)],
        block_outs(EXTRA) + [((EXTRA, PART), F32)],
        tokens,
        [pltpu.VMEM((ROWS, 128), F32)],
        flops=sum(2 * ROWS * MODEL * w.shape[1] for _, w in pairs),
    )


def norm_back(name, p0, sums, pieces, gain_part, rows, mean, inv, residual, low_out, tokens):
    def body(p0, sums, ra, rb, la, lb, gain, rows, mean, inv, residual, grad, gain_grad, *low):
        total = sums[...] + ra[HALF:].astype(F32) + la[HALF:].astype(F32)
        total = jnp.concatenate([total, jnp.zeros((128 - EXTRA, PART), F32)], axis=0).T
        acc = jnp.zeros((1, PART), F32)
        for half, (one, two) in enumerate(((ra, la), (rb, lb))):
            for quarter in range(2):
                at = slice(quarter * 128, (quarter + 1) * 128)
                out = slice(half * HALF + quarter * 128, half * HALF + (quarter + 1) * 128)
                g = p0[out] + one[at].astype(F32) + two[at].astype(F32)
                normed = (rows[out].astype(F32) - mean[out]) * inv[out]
                acc = acc + jnp.sum(g * normed, axis=0, keepdims=True)
                back = inv[out] * (g * gain[...] - total[out, 0:1] - normed * total[out, 1:2])
                new = residual[out].astype(F32) + back
                grad[out] = new
                if low_out:
                    low[half][at] = new.astype(BF16)
        gain_grad[...] = acc

    outs = [((ROWS, PART), F32), ((1, PART), F32)]
    if low_out:
        outs += [((HALF, PART), BF16)] * 2
    return call(
        name,
        body,
        (1,),
        [],
        [(p0,), (sums,)]
        + [(p,) for p in pieces]
        + [(gain_part,), (rows,), (mean,), (inv,), (residual,)],
        outs,
        tokens,
    )


def back_mix(info, parts, wo, gate, grouped, ginv, query, arrival, tokens):
    def body(info, *refs):
        parts = refs[:8]
        wo, gate, grouped, ginv, query, arrival, branch, grad_gate, kept, own, give = refs[8:]
        head = pl.program_id(0)

        @pl.when(head == 0)
        def _():
            for k in range(SIDE):
                cols = pl.ds(head_col(info, k), PART)
                branch[:HALF, cols] = parts[2 * k][...]
                branch[HALF:, cols] = parts[2 * k + 1][...]

        for half in range(2):
            rows = slice(half * HALF, (half + 1) * HALF)
            m = dot_t(branch[rows], wo[...])
            g = gate[rows]
            sigmoid = 1.0 / (1.0 + jnp.exp(-g))
            group = grouped[rows].astype(F32)
            slope = sigmoid * (1.0 + g * (1.0 - sigmoid))
            grad_gate[rows] = (m * group * slope).astype(BF16)
            e = m * (g * sigmoid)
            e = ginv[0, rows] * (
                e
                - jnp.mean(e, axis=1, keepdims=True)
                - group * jnp.mean(e * group, axis=1, keepdims=True)
            )
            kept[rows] = e.astype(BF16)
        moved = (query[...].astype(F32) * arrival[0]).astype(BF16)
        state = t_dot(moved, kept[...])

        @pl.when(head == info[1])
        def _():
            own[...] = state

        @pl.when(head != info[1])
        def _():
            give[...] = state.astype(BF16)

    by_head = lambda h, *_: (0, h)
    cube = lambda h, *_: (h, 0, 0)
    cols = HEADS * VAL
    return call(
        "back_mix",
        body,
        (HEADS,),
        [info],
        [(p,) for p in parts]
        + [
            (wo, (VAL, MODEL), lambda h, *_: (h, 0)),
            (gate, (ROWS, VAL), by_head),
            (grouped, (ROWS, VAL), by_head),
            (ginv, (1, ROWS, 1), cube),
            (query, (ROWS, KEY), by_head),
            (arrival, (1, ROWS, 1), cube),
        ],
        [
            ((ROWS, MODEL), BF16),
            ((ROWS, cols), BF16, (ROWS, VAL), by_head),
            ((ROWS, cols), BF16, (ROWS, VAL), by_head),
            ((KEY, VAL), F32),
            ((KEY, VAL), BF16),
        ],
        tokens,
        flops=2 * ROWS * MODEL * cols,
    )


def retain_back(info, kept, value, decay, key, query, weighted, mine, sibling, arrival, cosine, sine, tokens):
    def body(
        info, kept, value, decay, key, query, weighted, mine, sibling, arrival, cosine, sine,
        grad_query, near_key, near_value,
    ):
        head = pl.program_id(0)
        e = kept[...]
        s = (dot_t(e, value[...]) * decay[0]).astype(BF16)
        state = pick(mine, sibling, info, head)
        gq = dot(s, key[...]) + arrival[0] * dot_t(e, state)
        grad_query[...] = rotate(gq, cosine[...], -sine[...]).astype(BF16)
        near_key[...] = t_dot(s, query[...])
        near_value[...] = t_dot(weighted[0], e)

    by_head = lambda h, *_: (0, h)
    cube = lambda h, *_: (h, 0, 0)
    keys, vals = HEADS * KEY, HEADS * VAL
    return call(
        "retain_back",
        body,
        (HEADS,),
        [info],
        [
            (kept, (ROWS, VAL), by_head),
            (value, (ROWS, VAL), by_head),
            (decay, (1, ROWS, ROWS), cube),
            (key, (ROWS, KEY), by_head),
            (query, (ROWS, KEY), by_head),
            (weighted, (1, ROWS, ROWS), cube),
            (mine,),
            (sibling,),
            (arrival, (1, ROWS, 1), cube),
            (cosine,),
            (sine,),
        ],
        [
            ((ROWS, keys), BF16, (ROWS, KEY), by_head),
            ((ROWS, keys), F32, (ROWS, KEY), by_head),
            ((ROWS, vals), F32, (ROWS, VAL), by_head),
        ],
        tokens,
        flops=2 * HEADS * ROWS * ROWS * 1800,
    )


def key_value_back(info, mine, sibling, key, value, departure, near_key, near_value, cosine, sine, tokens):
    def body(
        info, mine, sibling, key, value, departure, near_key, near_value, cosine, sine,
        grad_key, grad_value,
    ):
        state = pick(mine, sibling, info, pl.program_id(0))
        gk = near_key[...] + departure[0] * dot_t(value[...], state)
        grad_key[...] = rotate(gk, cosine[...], -sine[...]).astype(BF16)
        gv = near_value[...] + departure[0] * dot(key[...], state)
        grad_value[...] = gv.astype(BF16)

    by_head = lambda h, *_: (0, h)
    keys, vals = HEADS * KEY, HEADS * VAL
    return call(
        "key_value_back",
        body,
        (HEADS,),
        [info],
        [
            (mine,),
            (sibling,),
            (key, (ROWS, KEY), by_head),
            (value, (ROWS, VAL), by_head),
            (departure, (1, ROWS, 1), lambda h, *_: (h, 0, 0)),
            (near_key, (ROWS, KEY), by_head),
            (near_value, (ROWS, VAL), by_head),
            (cosine,),
            (sine,),
        ],
        [
            ((ROWS, keys), BF16, (ROWS, KEY), by_head),
            ((ROWS, vals), BF16, (ROWS, VAL), by_head),
        ],
        tokens,
        flops=2 * HEADS * ROWS * KEY * VAL * 2,
    )


def turn(name, info, low, x_first, tokens=()):
    def body(info, low, own, other, scratch):
        scratch[...] = low[...].T
        for y in range(SIDE):
            base = y * CORES * 64
            mine = scratch[pl.ds(pl.multiple_of(base + info[1] * 64, 64), 64), :]
            far = scratch[pl.ds(pl.multiple_of(base + (1 - info[1]) * 64, 64), 64), :]
            if x_first:
                own[0, y] = mine
                other[0, y] = far
            else:
                own[y, 0] = mine
                other[y, 0] = far

    if x_first:
        out = ((SIDE, SIDE, 64, ROWS), BF16, (1, SIDE, 64, ROWS), lambda i, *_: (i, 0, 0, 0))
    else:
        out = ((SIDE, SIDE, 64, ROWS), BF16, (SIDE, 1, 64, ROWS), lambda i, *_: (0, i, 0, 0))
    own, other = call(
        name,
        body,
        (SIDE,),
        [info],
        [(low, (ROWS, PART), lambda i, *_: (0, i))],
        [out, out],
        tokens,
        [pltpu.VMEM((PART, ROWS), BF16)],
    )
    return own.reshape(-1, ROWS), other.reshape(-1, ROWS)


def weight_other(name, left, rights, tokens=()):
    n = len(rights)
    width = sum(r.shape[1] for r in rights)

    def body(left, *refs):
        out, at = refs[n], 0
        for r in refs[:n]:
            out[:, at : at + r.shape[1]] = dot(left[...], r[...]).astype(BF16)
            at += r.shape[1]

    return call(
        name,
        body,
        (SIDE,),
        [],
        [(left, (HALF, ROWS), lambda i, *_: (i, 0))] + [(r,) for r in rights],
        [((SIDE * HALF, width), BF16, (HALF, width), lambda i, *_: (i, 0))],
        tokens,
        flops=2 * SIDE * HALF * ROWS * width,
    )[0]


def weight_own(name, info, where, left, rights, arrived, tokens=()):
    n = len(rights)
    width = sum(r.shape[1] for r in rights)

    def body(info, left, *refs):
        arrived, outs, at = refs[n], refs[n + 1 :], 0
        step = pl.program_id(0)
        for r in refs[:n]:
            cols = slice(at, at + r.shape[1])
            total = dot(left[...], r[...]) + arrived[:, cols].astype(F32)
            for k in range(SIDE):

                @pl.when(step == k)
                def _():
                    outs[k][:, cols] = total.astype(outs[k].dtype)

            at += r.shape[1]

    block = lambda i, info: (lax.rem(info[where] + ORDER_OF(i), SIDE), 0)
    return call(
        name,
        body,
        (SIDE,),
        [info],
        [(left, (HALF, ROWS), block)]
        + [(r,) for r in rights]
        + [(arrived, (HALF, width), block)],
        [((HALF, width), BF16)] * 3 + [((HALF, width), F32)],
        tokens,
        flops=2 * SIDE * HALF * ROWS * width,
    )


def ORDER_OF(i):
    return jnp.where(i == 0, 2, jnp.where(i == 1, 1, jnp.where(i == 2, 3, 0)))


def phase_sum(name, info, where, base, received, tokens=()):
    width = base.shape[1]

    def body(info, base, a, b, c, *refs):
        outs, scratch = refs[:SIDE], refs[SIDE]
        scratch[...] = base[...] + a[...].astype(F32) + b[...].astype(F32) + c[...].astype(F32)
        for i, k in enumerate(ORDER):
            at = pl.multiple_of(lax.rem(info[where] + k, SIDE) * 64, 64)
            outs[i][...] = scratch[pl.ds(at, 64), :].astype(outs[i].dtype)

    return call(
        name,
        body,
        (1,),
        [info],
        [(base,)] + [(r,) for r in received],
        [((64, width), BF16)] * 3 + [((64, width), F32)],
        tokens,
        [pltpu.VMEM((HALF, width), F32)],
    )


def shift_of(along_x):
    return (lambda k: seq_shift(k, 0)) if along_x else (lambda k: seq_shift(0, k))


def send_blocks(blocks, along_x):
    shift = shift_of(along_x)
    return [lax.ppermute(b, "seq", shift(k)) for b, k in zip(blocks, ORDER[:3])]


X_AT, Y_AT = 6, 7


def weight_rest(name, info, blocks, x_first, tokens=()):
    received = send_blocks(blocks[:3], x_first)
    subs = phase_sum(name, info, Y_AT if x_first else X_AT, blocks[3], received, tokens)
    received = send_blocks(subs[:3], not x_first)
    return subs[3] + sum(r.astype(F32) for r in received)


def scan_weights(decay, place, reverse):
    x, y, _ = place
    rel = jnp.arange(SIDE)
    origin = lax.rem(y - rel + SIDE, SIDE)
    target = lax.rem(y + rel, SIDE)
    hops = jnp.arange(1, SIDE)
    if reverse:
        row = origin
        before, counts = SIDE * (SIDE - hops - 1), x + (SIDE - hops) < SIDE
        gap = origin[None, :] - target[:, None]
        carry = SIDE - 1 - target
    else:
        row = SIDE - 1 - origin
        before, counts = SIDE * (hops - 1), x >= hops
        gap = target[:, None] - origin[None, :]
        carry = target
    gap = gap.reshape(-1)
    power = jnp.concatenate([row, before, jnp.maximum(gap - 1, 0), carry]).astype(F32)
    keep = jnp.concatenate([row >= 0, counts, gap > 0, carry >= 0]).astype(F32)
    values = keep * jnp.exp(2.0 * jnp.log(decay) * power)
    return jnp.concatenate([decay[None], values, jnp.zeros((4,), F32)])


W_ROW, W_BEFORE, W_ANSWER, W_CARRY = 1, 5, 8, 24
QUARTER = KEY // SIDE


def state_scan(info, weights, own, give, reverse, tag):
    far = 1 if reverse else 0

    def start_body(info, w, own, got, p2, p1, p3, p0, scratch):
        a, b = own[...], got[...].astype(F32)
        scratch[...] = jnp.where(info[1] == far, w[0] * a + b, a + w[0] * b).astype(BF16)
        for k, out in zip(ORDER, (p2, p1, p3, p0)):
            at = pl.multiple_of(lax.rem(info[Y_AT] + k, SIDE) * QUARTER, QUARTER)
            out[...] = scratch[pl.ds(at, QUARTER), :]

    piece = ((QUARTER, VAL), BF16)
    got = lax.ppermute(give, "seq", SWAP)
    sent = call(
        "scan_start" + tag, start_body, (1,), [info, weights], [(own,), (got,)], [piece] * 4,
        scratch=[pltpu.VMEM((KEY, VAL), BF16)],
    )
    at2, at1, at3 = send_blocks(sent[:3], False)
    pieces = [sent[3], at1, at2, at3]

    def row_body(w, p0, p1, p2, p3, total):
        total[...] = sum(
            w[W_ROW + j] * p[...].astype(F32) for j, p in enumerate((p0, p1, p2, p3))
        ).astype(BF16)

    row = call("scan_row" + tag, row_body, (1,), [weights], [(p,) for p in pieces], [piece])[0]
    at2, at1, at3 = send_blocks([row] * 3, True)

    def answer_body(w, p0, p1, p2, p3, b1, b2, b3, *outs):
        p = [r[...].astype(F32) for r in (p0, p1, p2, p3)]
        before = sum(w[W_BEFORE + j] * r[...].astype(F32) for j, r in enumerate((b1, b2, b3)))
        for k, out in zip(ORDER, outs):
            total = w[W_CARRY + k] * before
            for j in range(SIDE):
                total = total + w[W_ANSWER + SIDE * k + j] * p[j]
            out[...] = total.astype(BF16)

    answers = call(
        "scan_answer" + tag, answer_body, (1,), [weights],
        [(p,) for p in pieces] + [(at1,), (at2,), (at3,)], [piece] * 4,
    )
    at2, at1, at3 = send_blocks(answers[:3], False)

    def end_body(info, w, b0, b1, b2, b3, own, got, mine, theirs, scratch):
        for k, b in enumerate((b0, b1, b2, b3)):
            at = pl.multiple_of(lax.rem(info[Y_AT] + SIDE - k, SIDE) * QUARTER, QUARTER)
            scratch[pl.ds(at, QUARTER), :] = b[...].astype(F32)
        chip = scratch[...]
        is_far = info[1] == far
        later = w[0] * chip + jnp.where(is_far, own[...], got[...].astype(F32))
        mine[...] = jnp.where(is_far, chip, later).astype(BF16)
        theirs[...] = jnp.where(is_far, later, chip).astype(BF16)

    state = ((KEY, VAL), BF16)
    mine, theirs = call(
        "scan_end" + tag, end_body, (1,), [info, weights],
        [(answers[3],), (at1,), (at2,), (at3,), (own,), (got,)], [state, state],
        scratch=[pltpu.VMEM((KEY, VAL), F32)],
    )
    return mine, lax.ppermute(theirs, "seq", SWAP)


def sum_seq(values):
    values = values + lax.ppermute(values, "seq", SWAP)
    for along_x in (True, False):
        shift = shift_of(along_x)
        values = values + sum(lax.ppermute(values, "seq", shift(k)) for k in (1, 2, 3))
    return values


def shards(layer_in, gain1, wq, wk, wv, wg, wo, gain2, w1, w2, starts, cotangent):
    seq_rank = lax.axis_index("seq")
    head_rank = lax.axis_index("head")
    x, y, core = (
        seq_rank // (SIDE * CORES),
        (seq_rank // CORES) % SIDE,
        seq_rank % CORES,
    )
    place = (x, y, core)
    info = jnp.stack(
        [head_rank, core] + [(head_rank + k) % SIDE for k in ORDER] + [x, y]
    ).astype(jnp.int32)
    col_start = head_rank * PART
    gain1_part = lax.dynamic_slice_in_dim(gain1, col_start, PART)[None]
    gain2_part = lax.dynamic_slice_in_dim(gain2, col_start, PART)[None]
    gain1, gain2 = gain1[None], gain2[None]

    offsets = jnp.arange(ROWS, dtype=jnp.int32)
    positions = seq_rank * ROWS + offsets
    member = positions[:, None] >= starts[None, :]
    doc_ids = jnp.sum(member.astype(jnp.int32), axis=-1) - 1
    last_start = jnp.max(jnp.where(member, starts[None, :], 0), axis=-1)
    relative = (positions - last_start).astype(F32)
    prior_doc = jnp.sum((seq_rank * ROWS - 1 >= starts).astype(jnp.int32)) - 1
    half_dim = KEY // 2
    frequency = jnp.exp(-math.log(10000.0) * jnp.arange(half_dim, dtype=F32) / half_dim)
    angles = relative[:, None] * frequency[None, :]
    cosine, sine = jnp.cos(angles), jnp.sin(angles)
    head_ids = (head_rank * HEADS + jnp.arange(HEADS, dtype=jnp.int32)).astype(F32)
    log_decay = jnp.log1p(-jnp.exp2(-5.0 - head_ids))
    gap_grid = offsets[:, None] - offsets[None, :]
    keep = (gap_grid >= 0) & (doc_ids[:, None] == doc_ids[None, :])
    gap_float = jnp.where(gap_grid >= 0, gap_grid, 0).astype(F32)
    decay = jnp.where(keep[None], jnp.exp(gap_float[None] * log_decay[:, None, None]), 0.0)
    step_float = offsets.astype(F32)
    arrival = jnp.exp((step_float[None, :] + 1.0) * log_decay[:, None]) * (
        doc_ids == prior_doc
    ).astype(F32)
    departure = jnp.exp((ROWS - 1.0 - step_float)[None, :] * log_decay[:, None]) * (
        doc_ids == doc_ids[ROWS - 1]
    ).astype(F32)
    arrival, departure = arrival[:, :, None], departure[:, :, None]
    rank_decay = lax.dynamic_index_in_dim(jnp.exp(ROWS * log_decay), core, 0, False)
    ahead = scan_weights(rank_decay, place, False)
    behind = scan_weights(rank_decay, place, True)

    x_parts = ring_gather(layer_in[:HALF], layer_in[HALF:])
    low1, mean1, inv1, cot_again = norm1(info, x_parts, gain1, cotangent)
    cot_full = lax.all_gather(cot_again, "head", axis=1, tiled=True)
    key, value, own, give = key_value(info, low1, wk, wv, cosine, sine, departure)
    mine, sibling = state_scan(info, ahead, own, give, False, "_a")
    query, weighted, within = query_part(low1, wq, key, value, decay, cosine, sine, ())
    gate = matmul_cols("gate", low1, wg, F32, (key,))
    mixed, grouped, ginv, *blocks = mix(info, within, gate, query, mine, sibling, arrival, wo)
    pieces = ring_scatter(*blocks[:6])
    grad_hidden = matmul_rows("grad_hidden", cot_full, w2, BF16, (blocks[0],))
    cot_own, cot_other = turn("turn_cot", info, cot_full, True, (blocks[0],))
    b_parts = ring_gather(*sum_branch(blocks[6], pieces))
    low1_own, low1_other = turn("turn_low1", info, low1, True, (b_parts[0],))

    low2, mean2, inv2, middle, hidden, grad_pre = feed_up(
        info, x_parts, b_parts, gain2, w1, grad_hidden, (cot_own, low1_own)
    )
    *blocks, sums = back_blocks("back_feed", info, [(grad_pre, w1)], None, gain2, low2)
    pieces = ring_scatter(*blocks[:6])
    w2_other = weight_other("w2_other", cot_other, [hidden], (blocks[0],))
    low2_own, low2_other = turn("turn_low2", info, low2, False, (blocks[0],))
    w1_other = weight_other("w1_other", low2_other, [grad_pre])
    w2_got, w1_got = lax.ppermute(w2_other, "seq", SWAP), lax.ppermute(w1_other, "seq", SWAP)
    grad_middle, gain2_grad, half_a, half_b = norm_back(
        "norm_back2", blocks[6], sums, pieces, gain2_part, middle, mean2, inv2, cotangent, True,
        (w1_other, w2_other),
    )
    g_parts = ring_gather(half_a, half_b)
    w2_blocks = weight_own("w2_own", info, X_AT, cot_own, [hidden], w2_got, (half_a,))
    w1_blocks = weight_own("w1_own", info, Y_AT, low2_own, [grad_pre], w1_got, (half_a,))

    branch, grad_gate, kept, own, give = back_mix(
        info, g_parts, wo, gate, grouped, ginv, query, arrival, (w2_blocks[0], w1_blocks[0])
    )
    far_mine, far_sibling = state_scan(info, behind, own, give, True, "_b")
    grad_query, near_key, near_value = retain_back(
        info, kept, value, decay, key, query, weighted, mine, sibling, arrival, cosine, sine, ()
    )
    grad_w2 = weight_rest("w2_mid", info, w2_blocks, True)
    grad_w1 = weight_rest("w1_mid", info, w1_blocks, False)
    feed = matmul_cols("feed_down", hidden, w2, BF16, (kept,))
    feed = lax.psum_scatter(feed, "head", scatter_dimension=1, tiled=True)
    branch_own, branch_other = turn("turn_branch", info, branch, False, ())
    wo_other = weight_other("wo_other", branch_other, [mixed])
    wg_other = weight_other("wg_other", low1_other, [grad_gate, grad_query])
    wo_got, wg_got = lax.ppermute(wo_other, "seq", SWAP), lax.ppermute(wg_other, "seq", SWAP)
    grad_key, grad_value = key_value_back(
        info, far_mine, far_sibling, key, value, departure, near_key, near_value, cosine, sine,
        (wo_other, wg_other),
    )
    wv_other = weight_other("wv_other", low1_other, [grad_value])
    wk_other = weight_other("wk_other", low1_other, [grad_key])
    wv_got, wk_got = lax.ppermute(wv_other, "seq", SWAP), lax.ppermute(wk_other, "seq", SWAP)
    *blocks, sums = back_blocks(
        "back_proj", info,
        [(grad_query, wq), (grad_gate, wg), (grad_key, wk), (grad_value, wv)],
        None, gain1, low1, (wv_other, wk_other),
    )
    pieces = ring_scatter(*blocks[:6])
    wo_blocks = weight_own("wo_own", info, Y_AT, branch_own, [mixed], wo_got)
    wg_blocks = weight_own("wg_own", info, X_AT, low1_own, [grad_gate, grad_query], wg_got)
    wv_blocks = weight_own("wv_own", info, X_AT, low1_own, [grad_value], wv_got)
    wk_blocks = weight_own("wk_own", info, X_AT, low1_own, [grad_key], wk_got)
    grad_x, gain1_grad = norm_back(
        "norm_back1", blocks[6], sums, pieces, gain1_part, layer_in, mean1, inv1, grad_middle,
        False, (),
    )
    grad_wo = weight_rest("wo_mid", info, wo_blocks, False)
    grad_wgq = weight_rest("wg_mid", info, wg_blocks, True)
    grad_wv = weight_rest("wv_mid", info, wv_blocks, True)
    grad_wk = weight_rest("wk_mid", info, wk_blocks, True)
    gains = sum_seq(jnp.concatenate([gain1_grad, gain2_grad], axis=0))
    output = (middle + feed.astype(F32)).astype(BF16)
    return (
        output,
        grad_x,
        gains[0],
        grad_wgq[:, HEADS * VAL :],
        grad_wk,
        grad_wv,
        grad_wgq[:, : HEADS * VAL],
        grad_wo.T,
        gains[1],
        grad_w1,
        grad_w2.T,
    )


def solution(mesh):
    rows = P("seq", "head")
    cols = P(None, "head")
    tall = P("head", None)
    return jax.shard_map(
        shards,
        mesh=mesh,
        in_specs=(rows, P(), cols, cols, cols, cols, tall, P(), cols, tall, P(), rows),
        out_specs=(
            rows, rows, P("head"), rows, rows, rows, rows, P("head", "seq"), P("head"), rows,
            P("head", "seq"),
        ),
        check_vma=False,
    )
```

time: 632 us -> 573 us (0.907)
  Pallas kernels: 0 us -> 158 us
  matrix products: 103 us -> 0 us
  blocking collectives: 67.7 us -> 0 us
  other arithmetic: 66.3 us -> 18.9 us
  starting transfers between devices: 119 us -> 140 us
  local copies, waits for them, and re-layouts: 72.7 us -> 62.5 us
  waiting for transfers between devices: 174 us -> 167 us
    pallas_call x0 -> x46, Pallas kernels: none -> 158 us  [call(): pl.pallas_call(run, name=name, grid_spec=pltpu.PrefetchScalarGridSpec(num...]
    dot_general x40 -> x0, matrix products: 103 us -> none  [the longest x19 59.1 us: dot(): return jnp.dot(left, right, preferred_element_type=F32)]
    psum x1 -> x0, blocking collectives: 67.7 us -> none  [shards(): gain1_total, gain2_total = lax.psum((gain1_grad, gain2_grad), 'seq')]
    unnamed x212 -> x288, local copies, waits for them, and re-layouts: 12.9 us -> 57.8 us
    ppermute x88 -> x107, starting transfers between devices: 118 us -> 140 us  [the longest x54 84.5 us: send_blocks(): return [lax.ppermute(b, 'seq', shift(k)) for b, k in zip(blocks, ORDER[:3])]]
    dynamic_slice x14 -> x3, local copies, waits for them, and re-layouts: 15.1 us -> 0.71 us  [the longest x1 0.55 us: shards(): lax.dynamic_index_in_dim(jnp.exp(ROWS * log_decay), core, 0, False)]
    reduce_sum x10 -> x2, other arithmetic: 16.2 us -> 2.04 us  [the longest x1 1.29 us: shards(): prior_doc = jnp.sum((seq_rank * ROWS - 1 >= starts).astype(jnp.int32)) - 1]
    dynamic_update_slice x18 -> x0, local copies, waits for them, and re-layouts: 12.7 us -> none  [the longest x10 12.6 us: assemble(): whole = lax.dynamic_update_slice(whole, part, (0, at * width))]
  transfers between devices with their start and end apart: 90 -> 109, of which waited for: 44 -> 43; matrix products, arithmetic and copies ran while one was open for 27% -> 4% of each run, Pallas kernels for 0% -> 22%
where the time goes in v2:
time: 573 us; the launch traced here: 563 us
  waiting for transfers between devices  167 us (29%)
  Pallas kernels  158 us (28%)
  starting transfers between devices  140 us (24%)
  local copies, waits for them, and re-layouts  62.5 us (11%)
  other arithmetic  18.9 us (3%)
  between operations  16.9 us (3%)
    pallas_call x46, Pallas kernels, call(): pl.pallas_call(run, name=name, grid_spec=pltpu.PrefetchScalarGridSpec(num...  158 us
    ppermute x54, waiting for transfers between devices, send_blocks(): return [lax.ppermute(b, 'seq', shift(k)) for b, k in zip(blocks, ORDER[:3])]  87.3 us
    ppermute x54, starting transfers between devices, send_blocks(): return [lax.ppermute(b, 'seq', shift(k)) for b, k in zip(blocks, ORDER[:3])]  84.5 us
    unnamed x288, local copies, waits for them, and re-layouts  57.8 us
    ppermute x18, starting transfers between devices, down(): return lax.ppermute(block, 'head', head_shift(SIDE - 1))  39.6 us
    ppermute x18, waiting for transfers between devices, up(): return lax.ppermute(block, 'head', head_shift(1))  39.2 us
    ppermute x18, waiting for transfers between devices, down(): return lax.ppermute(block, 'head', head_shift(SIDE - 1))  32.7 us
  transfers between devices with their start and end apart: 109, of which 43 were waited for; matrix products, arithmetic and copies ran while one was open for 4% of the time, Pallas kernels for 22%

profile of v2, /device:TPU:0, one launch (start us, length us, event | category | flops | bytes accessed | tf_op | source)
XLA Modules:
  0.0 563.5 jit_solution(3018291403185233434)
XLA Ops:
  44.6 5.0 norm1.1
  53.3 7.7 %key_value.1 = (bf16[512,512]{1,0:T(8,128)(2,1)S(1)}, bf16[512,1024]{1,0:T(8,128)(2,1)S(1)}, f32[256,512]{1,0:T(8,128)S(1)}, bf16[256,512]{1,0:T(8,128)(2,1)}) custom-call(s32[8]{0:T(128)S(1)} %stack.35.refs_0_, bf16[512,2048]{1,0:T(8,128)(2,1)S(1)} %get-tuple-element.148.refs_1_.refs_0_.refs_10_, bf16[2048,512]{1,0:T(8,128)(2,1)} %refs_7_.4, ...), custom_call_target="tpu_custom_call" | custom-call | flops 3221225472 | bytes 11276288 | tf_op jit(solution)/shard_map/key_value/pallas_call | solution.py:91
  95.3 6.4 %query_part.1 = (bf16[512,512]{1,0:T(8,128)(2,1)S(1)}, bf16[2,512,512]{2,1,0:T(8,128)(2,1)S(1)}, f32[512,1024]{1,0:T(8,128)S(1)}) custom-call(bf16[512,2048]{1,0:T(8,128)(2,1)} %copy-done, bf16[2048,512]{1,0:T(8,128)(2,1)} %refs_5_.1, bf16[512,512]{1,0:T(8,128)(2,1)S(1)} %copy-done.9, bf16[512,1024]{1,0:T(8,128)(2,1)S(1)} %get-tuple-element.150.refs_3_.refs_2_.refs_4_, ...), custom_call_target="tpu_custom_call" | custom-call | flops 1879048192 | bytes 12058624 | tf_op jit(solution)/shard_map/query_part/pallas_call | solution.py:91
  109.9 9.2 %mix.1 = (bf16[512,1024]{1,0:T(8,128)(2,1)S(1)}, bf16[512,1024]{1,0:T(8,128)(2,1)S(1)}, f32[2,512,1]{2,1,0:T(8,128)S(1)}, bf16[256,512]{1,0:T(8,128)(2,1)S(1)}, ...) custom-call(s32[8]{0:T(128)S(1)} %stack.35.refs_0_, ...), custom_call_target="tpu_custom_call" | custom-call | flops 2147483648 | bytes 14163968 | tf_op jit(solution)/shard_map/mix/pallas_call | solution.py:91
  162.1 5.0 grad_hidden.1.refs_19_
  168.1 10.9 %feed_up.1 = (bf16[512,2048]{1,0:T(8,128)(2,1)}, f32[512,1]{1,0:T(8,128)S(1)}, f32[512,1]{1,0:T(8,128)S(1)}, f32[512,512]{1,0:T(8,128)S(1)}, bf16[512,1024]{1,0:T(8,128)(2,1)}, /*index=5*/bf16[512,1024]{1,0:T(8,128)(2,1)}) custom-call(s32[8]{0:T(128)S(1)} %stack.35.refs_0_, bf16[256,512]{1,0:T(8,128)(2,1)S(1)} %copy-done.41, ...), custom_call_target="tpu_custom_call" | custom-call | flops 2147483648 | bytes 14692352 | tf_op jit(solution)/shard_map/feed_up/pallas_call | solution.py:91
  184.3 7.1 %back_feed.1 = (bf16[272,512]{1,0:T(8,128)(2,1)S(1)}, bf16[256,512]{1,0:T(8,128)(2,1)S(1)}, bf16[272,512]{1,0:T(8,128)(2,1)S(1)}, bf16[256,512]{1,0:T(8,128)(2,1...) custom-call(s32[8]{0:T(128)S(1)} %stack.35.refs_0_, ...), custom_call_target="tpu_custom_call" | custom-call | flops 2147483648 | bytes 10051584 | tf_op jit(solution)/shard_map/back_feed/pallas_call | solution.py:91
  203.7 7.5 %collective-permute-done.29 = bf16[272,512]{1,0:T(8,128)(2,1)S(1)} collective-permute-done((bf16[272,512]{1,0:T(8,128)(2,1)S(1)}, bf16[272,512]{1,0:T(8,128)(2,1)S(1)}, u32[]{:S(2)}, u32[]{:S(2)}) %collective-permute-start.29) | collective-permute-done | bytes 278560 | tf_op jit(solution)/shard_map/ppermute | solution.py:48
  219.1 5.3 collective-permute-done.34.refs_5_
  253.6 5.2 w1_own.1
  259.8 8.4 %back_mix.1 = (bf16[512,2048]{1,0:T(8,128)(2,1)}, bf16[512,1024]{1,0:T(8,128)(2,1)}, bf16[512,1024]{1,0:T(8,128)(2,1)}, f32[256,512]{1,0:T(8,128)S(1)}, bf16[256,512]{1,0:T(8,128)(2,1)S(1)}) custom-call(s32[8]{0:T(128)S(1)} %stack.35.refs_0_, bf16[256,512]{1,0:T(8,128)(2,1)S(1)} %get-tuple-element.193.refs_4_.refs_1_, ...), custom_call_target="tpu_custom_call" | custom-call | flops 2147483648 | bytes 14950400 | tf_op jit(solution)/shard_map/back_mix/pallas_call | solution.py:91
  299.1 6.5 %collective-permute-start.96 = (bf16[256,1024]{1,0:T(8,128)(2,1)}, bf16[256,1024]{1,0:T(8,128)(2,1)S(1)}, u32[]{:S(2)}, u32[]{:S(2)}) collective-permute-start(bf16[256,1024]{1,0:T(8,128)(2,1)} %get-tuple-element.272), channel_id=1, source_target_pairs={{0,8},{4,12},{8,16},{12,20},{16,24},{20,28},{24,0},{28,4},{32,40},... | collective-permute-start | bytes 1572872 | tf_op jit(solution)/shard_map/ppermute | solution.py:792
  309.2 5.7 %retain_back.1 = (bf16[512,512]{1,0:T(8,128)(2,1)S(1)}, f32[512,512]{1,0:T(8,128)S(1)}, f32[512,1024]{1,0:T(8,128)}) custom-call(s32[8]{0:T(128)S(1)} %stack.35.refs_0_, bf16[512,1024]{1,0:T(8,128)(2,1)S(1)} %copy-done.35, bf16[512,1024]{1,0:T(8,128)(2,1)} %copy-done.5, f32[2,512,512]{2,1,0:T(8,128)} %exponential_select_fusion.refs_4_.refs_3_, ...), custom_call_target="tpu_custom_call" | custom-call | flops 1887436800 | bytes 11014144 | tf_op jit(solution)/shard_map/retain_back/pallas_call | solution.py:91
  342.1 12.3 %back_proj.1 = (bf16[272,512]{1,0:T(8,128)(2,1)}, bf16[256,512]{1,0:T(8,128)(2,1)S(1)}, bf16[272,512]{1,0:T(8,128)(2,1)S(1)}, bf16[256,512]{1,0:T(8,128)(2,1)S(1...) custom-call(s32[8]{0:T(128)S(1)} %stack.35.refs_0_, ...), custom_call_target="tpu_custom_call" | custom-call | flops 6442450944 | bytes 20537344 | tf_op jit(solution)/shard_map/back_proj/pallas_call | solution.py:91
  360.0 5.8 %collective-permute-done.56.refs_3_ = bf16[256,512]{1,0:T(8,128)(2,1)S(1)} collective-permute-done((bf16[256,512]{1,0:T(8,128)(2,1)S(1)}, bf16[256,512]{1,0:T(8,128)(2,1)S(1)}, u32[]{:S(2)}, u32[]{:S(2)}) %collective-permute-start.56) | collective-permute-done | bytes 262176 | tf_op jit(solution)/shard_map/ppermute | solution.py:48
  369.8 5.7 %feed_down.1 = bf16[512,2048]{1,0:T(8,128)(2,1)} custom-call(bf16[512,1024]{1,0:T(8,128)(2,1)S(1)} %copy-done.7, bf16[1024,2048]{1,0:T(8,128)(2,1)} %refs_1_.7, bf16[512,1024]{1,0:T(8,128)(2,1)S(1)} %copy-done.35), custom_call_target="tpu_custom_call" | custom-call | flops 2147483648 | bytes 7340032 | tf_op jit(solution)/shard_map/feed_down/pallas_call | solution.py:91
  379.6 11.7 %collective-permute-done.59.refs_5_ = bf16[256,512]{1,0:T(8,128)(2,1)S(1)} collective-permute-done((bf16[256,512]{1,0:T(8,128)(2,1)S(1)}, bf16[256,512]{1,0:T(8,128)(2,1)S(1)}, u32[]{:S(2)}, u32[]{:S(2)}) %collective-permute-start.59) | collective-permute-done | bytes 262176 | tf_op jit(solution)/shard_map/ppermute | solution.py:52
  395.4 10.6 %collective-permute-done.55.refs_2_ = bf16[272,512]{1,0:T(8,128)(2,1)S(1)} collective-permute-done((bf16[272,512]{1,0:T(8,128)(2,1)S(1)}, bf16[272,512]{1,0:T(8,128)(2,1)S(1)}, u32[]{:S(2)}, u32[]{:S(2)}) %collective-permute-start.55) | collective-permute-done | bytes 278560 | tf_op jit(solution)/shard_map/ppermute | solution.py:48
  414.0 6.8 %collective-permute-done.99 = bf16[64,1024]{1,0:T(8,128)(2,1)S(1)} collective-permute-done((bf16[64,1024]{1,0:T(8,128)(2,1)S(1)}, bf16[64,1024]{1,0:T(8,128)(2,1)S(1)}, u32[]{:S(2)}, u32[]{:S(2)}) %collective-permute-start.99) | collective-permute-done | bytes 131104 | tf_op jit(solution)/shard_map/ppermute | solution.py:792
  432.8 5.7 %collective-permute-done.61 = f32[2,512]{1,0:T(2,128)S(1)} collective-permute-done((f32[2,512]{1,0:T(2,128)S(1)}, f32[2,512]{1,0:T(2,128)S(1)}, u32[]{:S(2)}, u32[]{:S(2)}) %collective-permute-start.61) | collective-permute-done | bytes 4128 | tf_op jit(solution)/shard_map/ppermute | solution.py:897
  456.0 8.4 %collective-permute-done.90.refs_3_ = bf16[256,1024]{1,0:T(8,128)(2,1)S(1)} collective-permute-done((bf16[256,1024]{1,0:T(8,128)(2,1)S(1)}, bf16[256,1024]{1,0:T(8,128)(2,1)S(1)}, u32[]{:S(2)}, u32[]{:S(2)}) %collective-permute-start.90) | collective-permute-done | bytes 524320 | tf_op jit(solution)/shard_map/ppermute | solution.py:792
  476.7 6.6 %wg_own.1 = (bf16[256,1536]{1,0:T(8,128)(2,1)S(1)}, bf16[256,1536]{1,0:T(8,128)(2,1)S(1)}, bf16[256,1536]{1,0:T(8,128)(2,1)S(1)}, f32[256,1536]{1,0:T(8,128)}) custom-call(s32[8]{0:T(128)S(1)} %stack.35.refs_0_, bf16[1024,512]{1,0:T(8,128)(2,1)S(1)} %bitcast.31, bf16[512,1024]{1,0:T(8,128)(2,1)S(1)} %copy-done.128, bf16[512,512]{1,0:T(8,128)(2,1)S(1)} %copy-done.132, ...), custom_call_target="tpu_custom_call" | custom-call | flops 1610612736 | bytes 9699328 | tf_op jit(solution)/shard_map/wg_own/pallas_call | solution.py:91
  495.2 21.7 %collective-permute-done.83.refs_3_ = bf16[256,1024]{1,0:T(8,128)(2,1)S(1)} collective-permute-done((bf16[256,1024]{1,0:T(8,128)(2,1)S(1)}, bf16[256,1024]{1,0:T(8,128)(2,1)S(1)}, u32[]{:S(2)}, u32[]{:S(2)}) %collective-permute-start.83) | collective-permute-done | bytes 524320 | tf_op jit(solution)/shard_map/ppermute | solution.py:792
  521.8 14.5 %collective-permute-done.93 = bf16[64,1024]{1,0:T(8,128)(2,1)S(1)} collective-permute-done((bf16[64,1024]{1,0:T(8,128)(2,1)S(1)}, bf16[64,1024]{1,0:T(8,128)(2,1)S(1)}, u32[]{:S(2)}, u32[]{:S(2)}) %collective-permute-start.93) | collective-permute-done | bytes 131104 | tf_op jit(solution)/shard_map/ppermute | solution.py:792
  (587 shorter events, 346.9 us)
Async XLA Ops:
  7.2 150.6 %all-gather.2.cloned.1.call-start = ((), (), s32[]{:S(2)}) async-start(), calls=%async_computation.1 | async-start | bytes 2621440 | tf_op jit(solution)/shard_map/all_gather | solution.py:949
  51.0 503.5 %reduce-scatter.2.cloned.1.call-start = ((), (), s32[]{:S(2)}) async-start(), calls=%async_computation.2 | async-start | bytes 2621440 | tf_op jit(solution)/shard_map/reduce_scatter | solution.py:988
  144.3 23.7 %collective-permute-start.24 = (bf16[256,512]{1,0:T(8,128)(2,1)S(1)}, bf16[256,512]{1,0:T(8,128)(2,1)S(1)}, u32[]{:S(2)}, u32[]{:S(2)}) collective-permute-start(bf16[256,512]{1,0:T(8,128)(2,1)S(1)} %get-tuple-element.173.refs_10_), channel_id=1, source_target_pairs={{0,1},{1,2},{2,3},{3,0},{4,5},{5,6},{6,7},{7,4},{8,9},{9,10},{10,1... | collective-permute-start | bytes 786440 | tf_op jit(solution)/shard_map/ppermute | solution.py:48
  195.3 51.7 %collective-permute-start.41 = (bf16[1024,1024]{1,0:T(8,128)(2,1)}, bf16[1024,1024]{1,0:T(8,128)(2,1)}, u32[]{:S(2)}, u32[]{:S(2)}) collective-permute-start(bf16[1024,1024]{1,0:T(8,128)(2,1)} %w2_other.1.refs_12_), channel_id=1, source_target_pairs={{0,4},{4,0},{8,12},{12,8},{16,20},{20,16},{24,28},{28,24},{32,36},... | collective-permute-start | bytes 6291464 | tf_op jit(solution)/shard_map/ppermute | solution.py:969
  199.9 53.6 %collective-permute-start.42 = (bf16[1024,1024]{1,0:T(8,128)(2,1)S(1)}, bf16[1024,1024]{1,0:T(8,128)(2,1)}, u32[]{:S(2)}, u32[]{:S(2)}) collective-permute-start(bf16[1024,1024]{1,0:T(8,128)(2,1)S(1)} %w1_other.1.refs_11_), channel_id=1, source_target_pairs={{0,4},{4,0},{8,12},{12,8},{16,20},{20,16},{24,28},{28,24},{32,36},... | collective-permute-start | bytes 6291464 | tf_op jit(solution)/shard_map/ppermute | solution.py:969
  236.6 23.2 %collective-permute-start.36 = (bf16[256,512]{1,0:T(8,128)(2,1)S(1)}, bf16[256,512]{1,0:T(8,128)(2,1)S(1)}, u32[]{:S(2)}, u32[]{:S(2)}) collective-permute-start(bf16[256,512]{1,0:T(8,128)(2,1)S(1)} %get-tuple-element.194.refs_2_), channel_id=1, source_target_pairs={{0,1},{1,2},{2,3},{3,0},{4,5},{5,6},{6,7},{7,4},{8,9},{9,10},{10,1... | collective-permute-start | bytes 786440 | tf_op jit(solution)/shard_map/ppermute | solution.py:48
  268.3 38.9 %collective-permute-start.102 = (bf16[256,1024]{1,0:T(8,128)(2,1)S(1)}, bf16[256,1024]{1,0:T(8,128)(2,1)S(1)}, u32[]{:S(2)}, u32[]{:S(2)}) collective-permute-start(bf16[256,1024]{1,0:T(8,128)(2,1)S(1)} %get-tuple-element.279), channel_id=1, source_target_pairs={{0,32},{4,36},{8,40},{12,44},{16,48},{20,52},{24,56},{28,60},{32,6... | collective-permute-start | bytes 1572872 | tf_op jit(solution)/shard_map/ppermute | solution.py:792
  268.4 39.6 %collective-permute-start.103 = (bf16[256,1024]{1,0:T(8,128)(2,1)S(1)}, bf16[256,1024]{1,0:T(8,128)(2,1)S(1)}, u32[]{:S(2)}, u32[]{:S(2)}) collective-permute-start(bf16[256,1024]{1,0:T(8,128)(2,1)S(1)} %get-tuple-element.280), channel_id=1, source_target_pairs={{0,96},{4,100},{8,104},{12,108},{16,112},{20,116},{24,120},{28,124... | collective-permute-start | bytes 1572872 | tf_op jit(solution)/shard_map/ppermute | solution.py:792
  289.4 36.4 %collective-permute-start.101 = (bf16[256,1024]{1,0:T(8,128)(2,1)S(1)}, bf16[256,1024]{1,0:T(8,128)(2,1)}, u32[]{:S(2)}, u32[]{:S(2)}) collective-permute-start(bf16[256,1024]{1,0:T(8,128)(2,1)S(1)} %get-tuple-element.197.refs_15_), channel_id=1, source_target_pairs={{0,64},{4,68},{8,72},{12,76},{16,80},{20,84},{24,88},{28,92},{32,9... | collective-permute-start | bytes 1572872 | tf_op jit(solution)/shard_map/ppermute | solution.py:792
  296.2 42.7 %collective-permute-start.95 = (bf16[256,1024]{1,0:T(8,128)(2,1)S(1)}, bf16[256,1024]{1,0:T(8,128)(2,1)S(1)}, u32[]{:S(2)}, u32[]{:S(2)}) collective-permute-start(bf16[256,1024]{1,0:T(8,128)(2,1)S(1)} %get-tuple-element.199.refs_16_), channel_id=1, source_target_pairs={{0,16},{4,20},{8,24},{12,28},{16,0},{20,4},{24,8},{28,12},{32,48},... | collective-permute-start | bytes 1572872 | tf_op jit(solution)/shard_map/ppermute | solution.py:792
  299.1 37.6 %collective-permute-start.96 = (bf16[256,1024]{1,0:T(8,128)(2,1)}, bf16[256,1024]{1,0:T(8,128)(2,1)S(1)}, u32[]{:S(2)}, u32[]{:S(2)}) collective-permute-start(bf16[256,1024]{1,0:T(8,128)(2,1)} %get-tuple-element.272), channel_id=1, source_target_pairs={{0,8},{4,12},{8,16},{12,20},{16,24},{20,28},{24,0},{28,4},{32,40},... | collective-permute-start | bytes 1572872 | tf_op jit(solution)/shard_map/ppermute | solution.py:792
  308.1 30.8 %collective-permute-start.97 = (bf16[256,1024]{1,0:T(8,128)(2,1)}, bf16[256,1024]{1,0:T(8,128)(2,1)}, u32[]{:S(2)}, u32[]{:S(2)}) collective-permute-start(bf16[256,1024]{1,0:T(8,128)(2,1)} %get-tuple-element.273), channel_id=1, source_target_pairs={{0,24},{4,28},{8,0},{12,4},{16,8},{20,12},{24,16},{28,20},{32,56},... | collective-permute-start | bytes 1572872 | tf_op jit(solution)/shard_map/ppermute | solution.py:792
  325.8 102.7 %collective-permute-start.88 = (bf16[1024,1024]{1,0:T(8,128)(2,1)S(1)}, bf16[1024,1024]{1,0:T(8,128)(2,1)}, u32[]{:S(2)}, u32[]{:S(2)}) collective-permute-start(bf16[1024,1024]{1,0:T(8,128)(2,1)S(1)} %wo_other.1.refs_10_), channel_id=1, source_target_pairs={{0,4},{4,0},{8,12},{12,8},{16,20},{20,16},{24,28},{28,24},{32,36},... | collective-permute-start | bytes 6291464 | tf_op jit(solution)/shard_map/ppermute | solution.py:992
  328.4 146.1 %collective-permute-start.67 = (bf16[1024,1536]{1,0:T(8,128)(2,1)}, bf16[1024,1536]{1,0:T(8,128)(2,1)}, u32[]{:S(2)}, u32[]{:S(2)}) collective-permute-start(bf16[1024,1536]{1,0:T(8,128)(2,1)} %wg_other.1.refs_11_), channel_id=1, source_target_pairs={{0,4},{4,0},{8,12},{12,8},{16,20},{20,16},{24,28},{28,24},{32,36},... | collective-permute-start | bytes 9437192 | tf_op jit(solution)/shard_map/ppermute | solution.py:992
  360.0 81.8 %collective-permute-start.81 = (bf16[1024,1024]{1,0:T(8,128)(2,1)}, bf16[1024,1024]{1,0:T(8,128)(2,1)}, u32[]{:S(2)}, u32[]{:S(2)}) collective-permute-start(bf16[1024,1024]{1,0:T(8,128)(2,1)} %wv_other.1.refs_11_), channel_id=1, source_target_pairs={{0,4},{4,0},{8,12},{12,8},{16,20},{20,16},{24,28},{28,24},{32,36},... | collective-permute-start | bytes 6291464 | tf_op jit(solution)/shard_map/ppermute | solution.py:999
  375.6 45.2 %collective-permute-start.74 = (bf16[1024,512]{1,0:T(8,128)(2,1)}, bf16[1024,512]{1,0:T(8,128)(2,1)S(1)}, u32[]{:S(2)}, u32[]{:S(2)}) collective-permute-start(bf16[1024,512]{1,0:T(8,128)(2,1)} %copy-done.91), channel_id=1, source_target_pairs={{0,4},{4,0},{8,12},{12,8},{16,20},{20,16},{24,28},{28,24},{32,36},... | collective-permute-start | bytes 3145736 | tf_op jit(solution)/shard_map/ppermute | solution.py:999
  438.6 25.8 %collective-permute-start.90 = (bf16[256,1024]{1,0:T(8,128)(2,1)S(1)}, bf16[256,1024]{1,0:T(8,128)(2,1)S(1)}, u32[]{:S(2)}, u32[]{:S(2)}) collective-permute-start(bf16[256,1024]{1,0:T(8,128)(2,1)S(1)} %get-tuple-element.265), channel_id=1, source_target_pairs={{0,8},{4,12},{8,16},{12,20},{16,24},{20,28},{24,0},{28,4},{32,40},... | collective-permute-start | bytes 1572872 | tf_op jit(solution)/shard_map/ppermute | solution.py:792
  440.4 24.5 %collective-permute-start.91 = (bf16[256,1024]{1,0:T(8,128)(2,1)S(1)}, bf16[256,1024]{1,0:T(8,128)(2,1)S(1)}, u32[]{:S(2)}, u32[]{:S(2)}) collective-permute-start(bf16[256,1024]{1,0:T(8,128)(2,1)S(1)} %get-tuple-element.266), channel_id=1, source_target_pairs={{0,24},{4,28},{8,0},{12,4},{16,8},{20,12},{24,16},{28,20},{32,56},... | collective-permute-start | bytes 1572872 | tf_op jit(solution)/shard_map/ppermute | solution.py:792
  465.0 26.3 %collective-permute-start.82 = (bf16[256,1024]{1,0:T(8,128)(2,1)S(1)}, bf16[256,1024]{1,0:T(8,128)(2,1)S(1)}, u32[]{:S(2)}, u32[]{:S(2)}) collective-permute-start(bf16[256,1024]{1,0:T(8,128)(2,1)S(1)} %get-tuple-element.255), channel_id=1, source_target_pairs={{0,64},{4,68},{8,72},{12,76},{16,80},{20,84},{24,88},{28,92},{32,9... | collective-permute-start | bytes 1572872 | tf_op jit(solution)/shard_map/ppermute | solution.py:792
  484.0 32.9 %collective-permute-start.83 = (bf16[256,1024]{1,0:T(8,128)(2,1)S(1)}, bf16[256,1024]{1,0:T(8,128)(2,1)S(1)}, u32[]{:S(2)}, u32[]{:S(2)}) collective-permute-start(bf16[256,1024]{1,0:T(8,128)(2,1)S(1)} %get-tuple-element.256), channel_id=1, source_target_pairs={{0,32},{4,36},{8,40},{12,44},{16,48},{20,52},{24,56},{28,60},{32,6... | collective-permute-start | bytes 1572872 | tf_op jit(solution)/shard_map/ppermute | solution.py:792
  484.3 32.6 %collective-permute-start.84 = (bf16[256,1024]{1,0:T(8,128)(2,1)S(1)}, bf16[256,1024]{1,0:T(8,128)(2,1)S(1)}, u32[]{:S(2)}, u32[]{:S(2)}) collective-permute-start(bf16[256,1024]{1,0:T(8,128)(2,1)S(1)} %get-tuple-element.257), channel_id=1, source_target_pairs={{0,96},{4,100},{8,104},{12,108},{16,112},{20,116},{24,120},{28,124... | collective-permute-start | bytes 1572872 | tf_op jit(solution)/shard_map/ppermute | solution.py:792
  487.3 50.9 %collective-permute-start.68 = (bf16[256,1536]{1,0:T(8,128)(2,1)S(1)}, bf16[256,1536]{1,0:T(8,128)(2,1)S(1)}, u32[]{:S(2)}, u32[]{:S(2)}) collective-permute-start(bf16[256,1536]{1,0:T(8,128)(2,1)S(1)} %get-tuple-element.239), channel_id=1, source_target_pairs={{0,64},{4,68},{8,72},{12,76},{16,80},{20,84},{24,88},{28,92},{32,9... | collective-permute-start | bytes 2359304 | tf_op jit(solution)/shard_map/ppermute | solution.py:792
  491.3 49.8 %collective-permute-start.69 = (bf16[256,1536]{1,0:T(8,128)(2,1)S(1)}, bf16[256,1536]{1,0:T(8,128)(2,1)S(1)}, u32[]{:S(2)}, u32[]{:S(2)}) collective-permute-start(bf16[256,1536]{1,0:T(8,128)(2,1)S(1)} %get-tuple-element.240), channel_id=1, source_target_pairs={{0,32},{4,36},{8,40},{12,44},{16,48},{20,52},{24,56},{28,60},{32,6... | collective-permute-start | bytes 2359304 | tf_op jit(solution)/shard_map/ppermute | solution.py:792
  491.3 49.8 %collective-permute-start.70 = (bf16[256,1536]{1,0:T(8,128)(2,1)S(1)}, bf16[256,1536]{1,0:T(8,128)(2,1)S(1)}, u32[]{:S(2)}, u32[]{:S(2)}) collective-permute-start(bf16[256,1536]{1,0:T(8,128)(2,1)S(1)} %get-tuple-element.241), channel_id=1, source_target_pairs={{0,96},{4,100},{8,104},{12,108},{16,112},{20,116},{24,120},{28,124... | collective-permute-start | bytes 2359304 | tf_op jit(solution)/shard_map/ppermute | solution.py:792
  (229 other events, 2193.5 us)
Sparse Core Ops, SparseCore 0:
  51.1 29.9 all-gather.1
  375.7 31.5 reduce-scatter.1

commit v3 on v2

--- a/solution.py
+++ b/solution.py
@@ -20,7 +20,7 @@
 EPSILON = 1e-05
 F32 = jnp.float32
 BF16 = jnp.bfloat16
-VMEM_BYTES = 48 * 1024 * 1024
+VMEM_BYTES = 24 * 1024 * 1024
 ORDER = (2, 1, 3, 0)
 
 
@@ -56,6 +56,13 @@
     return (a.astype(F32) + b.astype(F32)).astype(BF16)
 
 
+def late(value, tokens):
+    def body(value, out):
+        out[...] = value[...]
+
+    return call("late", body, (1,), [], [(value,)], [(value.shape, value.dtype)], tokens)[0]
+
+
 def ring_gather(a, b):
     r1, l1 = up(a), down(b)
     r2, l2 = up(b), down(a)
@@ -66,17 +73,51 @@
 def ring_scatter(p2a, p2b, p1a, p1b, pma, pmb):
     t1, t2 = up(p2a), down(p2b)
     rb, la = up(p1b), down(pma)
-    ra, lb = up(add_low(p1a, t1)), down(add_low(pmb, t2))
-    return [ra, rb, la, lb]
+    s1, s2 = add_low(p1a, t1), add_low(pmb, t2)
+    ra, lb = up(s1), down(s2)
+    return [ra, rb, la, lb], (s1, s2)
 
 
 def whole(shape):
     return pl.BlockSpec(shape, lambda *_: (0,) * len(shape))
 
 
-def call(name, body, grid, scalars, ins, outs, tokens=(), scratch=(), flops=0):
+def once(shape):
+    return pl.BlockSpec(
+        shape, lambda *_: (0,) * len(shape), pipeline_mode=pl.Buffered(buffer_count=1)
+    )
+
+
+COST_SCALE = 1.0
+COSTS = {
+    "norm1": 5,
+    "key_value": 8,
+    "query_part": 6,
+    "gate": 4,
+    "mix": 9,
+    "grad_hidden": 5,
+    "feed_up": 11,
+    "back_feed": 7,
+    "back_mix": 8,
+    "retain_back": 6,
+    "feed_down": 5,
+    "key_value_back": 3,
+    "back_proj": 12,
+    "w2_other": 3,
+    "wg_other": 4,
+    "w2_own": 4,
+    "w1_own": 4,
+    "wo_own": 4,
+    "wg_own": 6,
+    "wv_own": 4,
+    "norm_back1": 3,
+    "norm_back2": 2,
+}
+
+
+def call(name, body, grid, scalars, ins, outs, tokens=(), scratch=()):
     arrays = [item[0] for item in ins]
-    in_specs = [whole(i[0].shape) if len(i) == 1 else pl.BlockSpec(i[1], i[2]) for i in ins]
+    in_specs = [once(i[0].shape) if len(i) == 1 else pl.BlockSpec(i[1], i[2]) for i in ins]
     out_specs = [whole(o[0]) if len(o) == 2 else pl.BlockSpec(o[2], o[3]) for o in outs]
     out_shape = [jax.ShapeDtypeStruct(o[0], o[1]) for o in outs]
     n_in, n_tok, n_sc = len(arrays), len(tokens), len(scalars)
@@ -85,9 +126,6 @@
     def run(*refs):
         body(*refs[: n_sc + n_in], *refs[n_sc + n_in + n_tok :])
 
-    moved = sum(a.size * a.dtype.itemsize for a in arrays) + sum(
-        math.prod(o[0]) * jnp.dtype(o[1]).itemsize for o in outs
-    )
     return pl.pallas_call(
         run,
         name=name,
@@ -102,7 +140,11 @@
         compiler_params=pltpu.CompilerParams(
             dimension_semantics=("arbitrary",) * len(grid), vmem_limit_bytes=VMEM_BYTES
         ),
-        cost_estimate=pl.CostEstimate(flops=flops, bytes_accessed=moved, transcendentals=0),
+        cost_estimate=pl.CostEstimate(
+            flops=int(COSTS.get(name, 1.5) * COST_SCALE * 1.1e9),
+            bytes_accessed=0,
+            transcendentals=0,
+        ),
     )(*scalars, *arrays, *tokens)
 
 
@@ -220,7 +262,6 @@
             ((KEY, VAL), F32),
             ((KEY, VAL), BF16),
         ],
-        flops=2 * ROWS * MODEL * 1536,
     )
 
 
@@ -254,7 +295,6 @@
             ((ROWS, HEADS * VAL), F32, (ROWS, VAL), by_head),
         ],
         tokens,
-        flops=2 * ROWS * MODEL * 512 + 4 * ROWS * ROWS * 768,
     )
 
 
@@ -272,7 +312,6 @@
         [(left,), (right, (depth, block), by_col)],
         [((left.shape[0], cols), out_type, (left.shape[0], block), by_col)],
         tokens,
-        flops=2 * left.shape[0] * depth * cols,
     )[0]
 
 
@@ -289,7 +328,6 @@
         [(left,), (right, (block, depth), lambda i, *_: (i, 0))],
         [((left.shape[0], cols), out_type, (left.shape[0], block), lambda i, *_: (0, i))],
         tokens,
-        flops=2 * left.shape[0] * depth * cols,
     )[0]
 
 
@@ -323,7 +361,7 @@
     return jnp.where(info[1] == head, mine[...], sibling[...])
 
 
-def mix(info, within, gate, query, mine, sibling, arrival, wo):
+def mix(info, within, gate, query, mine, sibling, arrival, wo, tokens):
     def body(info, within, gate, query, mine, sibling, arrival, wo, mixed, grouped, ginv, *outs):
         step = pl.program_id(0)
 
@@ -362,11 +400,11 @@
             (wo, (cols, PART), lambda i, info: (0, info[2 + i])),
         ],
         [((ROWS, cols), BF16), ((ROWS, cols), BF16), ((HEADS, ROWS, 1), F32)] + block_outs(0),
-        flops=2 * ROWS * MODEL * cols,
-    )
-
-
-def sum_branch(p0, pieces):
+        tokens,
+    )
+
+
+def sum_branch(p0, pieces, tokens):
     def body(p0, ra, rb, la, lb, a, b):
         a[...] = (p0[:HALF] + ra[...].astype(F32) + la[...].astype(F32)).astype(BF16)
         b[...] = (p0[HALF:] + rb[...].astype(F32) + lb[...].astype(F32)).astype(BF16)
@@ -378,6 +416,7 @@
         [],
         [(p0,)] + [(p,) for p in pieces],
         [((HALF, PART), BF16), ((HALF, PART), BF16)],
+        tokens,
     )
 
 
@@ -426,7 +465,6 @@
             tall,
         ],
         tokens,
-        flops=2 * ROWS * MODEL * cols,
     )
 
 
@@ -481,7 +519,6 @@
         block_outs(EXTRA) + [((EXTRA, PART), F32)],
         tokens,
         [pltpu.VMEM((ROWS, 128), F32)],
-        flops=sum(2 * ROWS * MODEL * w.shape[1] for _, w in pairs),
     )
 
 
@@ -584,7 +621,6 @@
             ((KEY, VAL), BF16),
         ],
         tokens,
-        flops=2 * ROWS * MODEL * cols,
     )
 
 
@@ -629,7 +665,6 @@
             ((ROWS, vals), F32, (ROWS, VAL), by_head),
         ],
         tokens,
-        flops=2 * HEADS * ROWS * ROWS * 1800,
     )
 
 
@@ -667,7 +702,6 @@
             ((ROWS, vals), BF16, (ROWS, VAL), by_head),
         ],
         tokens,
-        flops=2 * HEADS * ROWS * KEY * VAL * 2,
     )
 
 
@@ -720,7 +754,6 @@
         [(left, (HALF, ROWS), lambda i, *_: (i, 0))] + [(r,) for r in rights],
         [((SIDE * HALF, width), BF16, (HALF, width), lambda i, *_: (i, 0))],
         tokens,
-        flops=2 * SIDE * HALF * ROWS * width,
     )[0]
 
 
@@ -753,8 +786,54 @@
         + [(arrived, (HALF, width), block)],
         [((HALF, width), BF16)] * 3 + [((HALF, width), F32)],
         tokens,
-        flops=2 * SIDE * HALF * ROWS * width,
-    )
+    )
+
+
+def weight_whole(name, left, rights, arrived, tokens=()):
+    n = len(rights)
+    width = sum(r.shape[1] for r in rights)
+
+    def body(left, *refs):
+        arrived, out, at = refs[n], refs[n + 1], 0
+        for r in refs[:n]:
+            cols = slice(at, at + r.shape[1])
+            out[:, cols] = (dot(left[...], r[...]) + arrived[:, cols].astype(F32)).astype(BF16)
+            at += r.shape[1]
+
+    block = lambda i, *_: (i, 0)
+    return call(
+        name,
+        body,
+        (SIDE,),
+        [],
+        [(left, (HALF, ROWS), block)]
+        + [(r,) for r in rights]
+        + [(arrived, (HALF, width), block)],
+        [((SIDE * HALF, width), BF16, (HALF, width), block)],
+        tokens,
+    )[0]
+
+
+def axis_groups(along_x):
+    if along_x:
+        return [
+            [seq_index(x, y, c) for x in range(SIDE)] for y in range(SIDE) for c in range(CORES)
+        ]
+    return [[seq_index(x, y, c) for y in range(SIDE)] for x in range(SIDE) for c in range(CORES)]
+
+
+def weight_scatter(total, x_first):
+    steps = []
+    for along_x in (x_first, not x_first):
+        total = lax.psum_scatter(
+            total,
+            "seq",
+            scatter_dimension=0,
+            axis_index_groups=axis_groups(along_x),
+            tiled=True,
+        )
+        steps.append(total)
+    return total.astype(F32), steps[0]
 
 
 def ORDER_OF(i):
@@ -829,7 +908,7 @@
 QUARTER = KEY // SIDE
 
 
-def state_scan(info, weights, own, give, reverse, tag):
+def state_scan(info, weights, own, give, reverse, tag, fills):
     far = 1 if reverse else 0
 
     def start_body(info, w, own, got, p2, p1, p3, p0, scratch):
@@ -843,7 +922,7 @@
     got = lax.ppermute(give, "seq", SWAP)
     sent = call(
         "scan_start" + tag, start_body, (1,), [info, weights], [(own,), (got,)], [piece] * 4,
-        scratch=[pltpu.VMEM((KEY, VAL), BF16)],
+        fills[0](), scratch=[pltpu.VMEM((KEY, VAL), BF16)],
     )
     at2, at1, at3 = send_blocks(sent[:3], False)
     pieces = [sent[3], at1, at2, at3]
@@ -853,7 +932,10 @@
             w[W_ROW + j] * p[...].astype(F32) for j, p in enumerate((p0, p1, p2, p3))
         ).astype(BF16)
 
-    row = call("scan_row" + tag, row_body, (1,), [weights], [(p,) for p in pieces], [piece])[0]
+    row = call(
+        "scan_row" + tag, row_body, (1,), [weights], [(p,) for p in pieces], [piece],
+        fills[1](sent[0]),
+    )[0]
     at2, at1, at3 = send_blocks([row] * 3, True)
 
     def answer_body(w, p0, p1, p2, p3, b1, b2, b3, *outs):
@@ -867,7 +949,7 @@
 
     answers = call(
         "scan_answer" + tag, answer_body, (1,), [weights],
-        [(p,) for p in pieces] + [(at1,), (at2,), (at3,)], [piece] * 4,
+        [(p,) for p in pieces] + [(at1,), (at2,), (at3,)], [piece] * 4, fills[2](row),
     )
     at2, at1, at3 = send_blocks(answers[:3], False)
 
@@ -885,7 +967,7 @@
     mine, theirs = call(
         "scan_end" + tag, end_body, (1,), [info, weights],
         [(answers[3],), (at1,), (at2,), (at3,), (own,), (got,)], [state, state],
-        scratch=[pltpu.VMEM((KEY, VAL), F32)],
+        fills[3](answers[0]), scratch=[pltpu.VMEM((KEY, VAL), F32)],
     )
     return mine, lax.ppermute(theirs, "seq", SWAP)
 
@@ -915,6 +997,8 @@
     gain2_part = lax.dynamic_slice_in_dim(gain2, col_start, PART)[None]
     gain1, gain2 = gain1[None], gain2[None]
 
+    x_parts = ring_gather(layer_in[:HALF], layer_in[HALF:])
+    starts = late(starts[None], (x_parts[2], x_parts[7]))[0]
     offsets = jnp.arange(ROWS, dtype=jnp.int32)
     positions = seq_rank * ROWS + offsets
     member = positions[:, None] >= starts[None, :]
@@ -944,27 +1028,44 @@
     ahead = scan_weights(rank_decay, place, False)
     behind = scan_weights(rank_decay, place, True)
 
-    x_parts = ring_gather(layer_in[:HALF], layer_in[HALF:])
     low1, mean1, inv1, cot_again = norm1(info, x_parts, gain1, cotangent)
     cot_full = lax.all_gather(cot_again, "head", axis=1, tiled=True)
     key, value, own, give = key_value(info, low1, wk, wv, cosine, sine, departure)
-    mine, sibling = state_scan(info, ahead, own, give, False, "_a")
-    query, weighted, within = query_part(low1, wq, key, value, decay, cosine, sine, ())
-    gate = matmul_cols("gate", low1, wg, F32, (key,))
-    mixed, grouped, ginv, *blocks = mix(info, within, gate, query, mine, sibling, arrival, wo)
-    pieces = ring_scatter(*blocks[:6])
-    grad_hidden = matmul_rows("grad_hidden", cot_full, w2, BF16, (blocks[0],))
-    cot_own, cot_other = turn("turn_cot", info, cot_full, True, (blocks[0],))
-    b_parts = ring_gather(*sum_branch(blocks[6], pieces))
-    low1_own, low1_other = turn("turn_low1", info, low1, True, (b_parts[0],))
+    made = {}
+
+    def fill_query():
+        made["q"] = query_part(low1, wq, key, value, decay, cosine, sine, (give,))
+        return (made["q"][0],)
+
+    def fill_gate(token):
+        made["gate"] = matmul_cols("gate", low1, wg, F32, (token,))
+        return (made["gate"],)
+
+    def fill_turn(token):
+        made["low1_t"] = turn("turn_low1", info, low1, True, (token,))
+        return (made["low1_t"][0],)
+
+    mine, sibling = state_scan(
+        info, ahead, own, give, False, "_a", (fill_query, fill_gate, fill_turn, lambda token: ())
+    )
+    query, weighted, within = made["q"]
+    gate = made["gate"]
+    low1_own, low1_other = made["low1_t"]
+    mixed, grouped, ginv, *blocks = mix(
+        info, within, gate, query, mine, sibling, arrival, wo, (cot_full,)
+    )
+    pieces, sent = ring_scatter(*blocks[:6])
+    cot_own, cot_other = turn("turn_cot", info, cot_full, True, sent)
+    grad_hidden = matmul_rows("grad_hidden", cot_full, w2, BF16, (*sent, cot_own))
+    b_parts = ring_gather(*sum_branch(blocks[6], pieces, (grad_hidden,)))
 
     low2, mean2, inv2, middle, hidden, grad_pre = feed_up(
-        info, x_parts, b_parts, gain2, w1, grad_hidden, (cot_own, low1_own)
+        info, x_parts, b_parts, gain2, w1, grad_hidden, (cot_own,)
     )
     *blocks, sums = back_blocks("back_feed", info, [(grad_pre, w1)], None, gain2, low2)
-    pieces = ring_scatter(*blocks[:6])
-    w2_other = weight_other("w2_other", cot_other, [hidden], (blocks[0],))
-    low2_own, low2_other = turn("turn_low2", info, low2, False, (blocks[0],))
+    pieces, sent = ring_scatter(*blocks[:6])
+    w2_other = weight_other("w2_other", cot_other, [hidden], sent)
+    low2_own, low2_other = turn("turn_low2", info, low2, False, (*sent, w2_other))
     w1_other = weight_other("w1_other", low2_other, [grad_pre])
     w2_got, w1_got = lax.ppermute(w2_other, "seq", SWAP), lax.ppermute(w1_other, "seq", SWAP)
     grad_middle, gain2_grad, half_a, half_b = norm_back(
@@ -972,27 +1073,43 @@
         (w1_other, w2_other),
     )
     g_parts = ring_gather(half_a, half_b)
-    w2_blocks = weight_own("w2_own", info, X_AT, cot_own, [hidden], w2_got, (half_a,))
-    w1_blocks = weight_own("w1_own", info, Y_AT, low2_own, [grad_pre], w1_got, (half_a,))
+    sent = (g_parts[2], g_parts[7])
+    w2_total = weight_whole("w2_own", cot_own, [hidden], w2_got, sent)
+    w1_total = weight_whole("w1_own", low2_own, [grad_pre], w1_got, (*sent, w2_total))
+    grad_w2, w2_step = weight_scatter(w2_total, True)
+    grad_w1, w1_step = weight_scatter(w1_total, False)
 
     branch, grad_gate, kept, own, give = back_mix(
-        info, g_parts, wo, gate, grouped, ginv, query, arrival, (w2_blocks[0], w1_blocks[0])
-    )
-    far_mine, far_sibling = state_scan(info, behind, own, give, True, "_b")
-    grad_query, near_key, near_value = retain_back(
-        info, kept, value, decay, key, query, weighted, mine, sibling, arrival, cosine, sine, ()
-    )
-    grad_w2 = weight_rest("w2_mid", info, w2_blocks, True)
-    grad_w1 = weight_rest("w1_mid", info, w1_blocks, False)
-    feed = matmul_cols("feed_down", hidden, w2, BF16, (kept,))
-    feed = lax.psum_scatter(feed, "head", scatter_dimension=1, tiled=True)
-    branch_own, branch_other = turn("turn_branch", info, branch, False, ())
-    wo_other = weight_other("wo_other", branch_other, [mixed])
-    wg_other = weight_other("wg_other", low1_other, [grad_gate, grad_query])
-    wo_got, wg_got = lax.ppermute(wo_other, "seq", SWAP), lax.ppermute(wg_other, "seq", SWAP)
+        info, g_parts, wo, gate, grouped, ginv, query, arrival, (w2_total, w1_total)
+    )
+
+    def fill_feed(token):
+        made["feed"] = matmul_cols("feed_down", hidden, w2, BF16, (token,))
+        return (made["feed"],)
+
+    def fill_retain(token):
+        made["r"] = retain_back(
+            info, kept, value, decay, key, query, weighted, mine, sibling, arrival, cosine, sine,
+            (token,),
+        )
+        return (made["r"][0],)
+
+    def fill_wo(token):
+        made["branch_t"] = turn("turn_branch", info, branch, False, (token,))
+        made["wo"] = weight_other("wo_other", made["branch_t"][1], [mixed])
+        return (made["wo"],)
+
+    far_mine, far_sibling = state_scan(
+        info, behind, own, give, True, "_b", (lambda: (), fill_feed, fill_retain, fill_wo)
+    )
+    wg_other = weight_other("wg_other", low1_other, [grad_gate, made["r"][0]], (far_mine,))
+    branch_own, _ = made["branch_t"]
+    grad_query, near_key, near_value = made["r"]
+    feed = lax.psum_scatter(made["feed"], "head", scatter_dimension=1, tiled=True)
+    wo_got, wg_got = lax.ppermute(made["wo"], "seq", SWAP), lax.ppermute(wg_other, "seq", SWAP)
     grad_key, grad_value = key_value_back(
         info, far_mine, far_sibling, key, value, departure, near_key, near_value, cosine, sine,
-        (wo_other, wg_other),
+        (wg_other,),
     )
     wv_other = weight_other("wv_other", low1_other, [grad_value])
     wk_other = weight_other("wk_other", low1_other, [grad_key])
@@ -1000,19 +1117,25 @@
     *blocks, sums = back_blocks(
         "back_proj", info,
         [(grad_query, wq), (grad_gate, wg), (grad_key, wk), (grad_value, wv)],
-        None, gain1, low1, (wv_other, wk_other),
-    )
-    pieces = ring_scatter(*blocks[:6])
-    wo_blocks = weight_own("wo_own", info, Y_AT, branch_own, [mixed], wo_got)
-    wg_blocks = weight_own("wg_own", info, X_AT, low1_own, [grad_gate, grad_query], wg_got)
-    wv_blocks = weight_own("wv_own", info, X_AT, low1_own, [grad_value], wv_got)
-    wk_blocks = weight_own("wk_own", info, X_AT, low1_own, [grad_key], wk_got)
+        None, gain1, low1, (wv_other, wk_other, feed),
+    )
+    pieces, sent = ring_scatter(*blocks[:6])
+    wo_total = weight_whole("wo_own", branch_own, [mixed], wo_got, sent)
+    wg_total = weight_whole(
+        "wg_own", low1_own, [grad_gate, grad_query], wg_got, (*sent, wo_total)
+    )
+    wv_blocks = weight_own(
+        "wv_own", info, X_AT, low1_own, [grad_value], wv_got, (*sent, wg_total)
+    )
+    wk_blocks = weight_own(
+        "wk_own", info, X_AT, low1_own, [grad_key], wk_got, (*sent, wv_blocks[0])
+    )
     grad_x, gain1_grad = norm_back(
         "norm_back1", blocks[6], sums, pieces, gain1_part, layer_in, mean1, inv1, grad_middle,
-        False, (),
-    )
-    grad_wo = weight_rest("wo_mid", info, wo_blocks, False)
-    grad_wgq = weight_rest("wg_mid", info, wg_blocks, True)
+        False, (wo_total, wg_total, wv_blocks[0], wk_blocks[0]),
+    )
+    grad_wo, wo_step = weight_scatter(wo_total, False)
+    grad_wgq, wgq_step = weight_scatter(wg_total, True)
     grad_wv = weight_rest("wv_mid", info, wv_blocks, True)
     grad_wk = weight_rest("wk_mid", info, wk_blocks, True)
     gains = sum_seq(jnp.concatenate([gain1_grad, gain2_grad], axis=0))

time: 573 us -> 577 us (level)
  waiting for transfers between devices: 167 us -> 212 us
  starting transfers between devices: 140 us -> 108 us
  Pallas kernels: 158 us -> 129 us
  local copies, waits for them, and re-layouts: 62.5 us -> 85.1 us
    reduce_scatter x1 -> x9, waiting for transfers between devices: 0.01 us -> 98.5 us  [the longest x8 98.5 us: weight_scatter(): lax.psum_scatter(total, 'seq', scatter_dimension=0, axis_index_groups=axi...]
    ppermute x54 -> x30, waiting for transfers between devices: 87.3 us -> 15 us  [send_blocks(): return [lax.ppermute(b, 'seq', shift(k)) for b, k in zip(blocks, ORDER[:3])]]
    ppermute x54 -> x30, starting transfers between devices: 84.5 us -> 45.3 us  [send_blocks(): return [lax.ppermute(b, 'seq', shift(k)) for b, k in zip(blocks, ORDER[:3])]]
    pallas_call x46 -> x43, Pallas kernels: 158 us -> 129 us  [call(): pl.pallas_call(run, name=name, grid_spec=pltpu.PrefetchScalarGridSpec(num...]
    unnamed x288 -> x272, local copies, waits for them, and re-layouts: 57.8 us -> 77.8 us
    ppermute x6, waiting for transfers between devices: 6.2 us -> 18.9 us  [sum_seq(): lax.ppermute(values, 'seq', shift(k))]
    ppermute x18, waiting for transfers between devices: 32.7 us -> 21.6 us  [down(): return lax.ppermute(block, 'head', head_shift(SIDE - 1))]
    ppermute x18, waiting for transfers between devices: 39.2 us -> 45.7 us  [up(): return lax.ppermute(block, 'head', head_shift(1))]
  transfers between devices with their start and end apart: 109 -> 93, of which waited for: 43 -> 36; matrix products, arithmetic and copies ran while one was open for 4% -> 3% of each run, Pallas kernels for 22% -> 15%
where the time goes in v3:
time: 577 us; the launch traced here: 567 us
  waiting for transfers between devices  212 us (37%)
  Pallas kernels  129 us (22%)
  starting transfers between devices  108 us (19%)
  local copies, waits for them, and re-layouts  85.1 us (15%)
  between operations  17.5 us (3%)
  other arithmetic  15.4 us (3%)
    pallas_call x43, Pallas kernels, call(): pl.pallas_call(run, name=name, grid_spec=pltpu.PrefetchScalarGridSpec(num...  129 us
    reduce_scatter x8, waiting for transfers between devices, weight_scatter(): lax.psum_scatter(total, 'seq', scatter_dimension=0, axis_index_groups=axi...  98.5 us
    unnamed x272, local copies, waits for them, and re-layouts  77.8 us
    ppermute x18, waiting for transfers between devices, up(): return lax.ppermute(block, 'head', head_shift(1))  45.7 us
    ppermute x30, starting transfers between devices, send_blocks(): return [lax.ppermute(b, 'seq', shift(k)) for b, k in zip(blocks, ORDER[:3])]  45.3 us
    ppermute x18, starting transfers between devices, down(): return lax.ppermute(block, 'head', head_shift(SIDE - 1))  44.7 us
    ppermute x18, waiting for transfers between devices, down(): return lax.ppermute(block, 'head', head_shift(SIDE - 1))  21.6 us
    ppermute x6, waiting for transfers between devices, sum_seq(): lax.ppermute(values, 'seq', shift(k))  18.9 us
  transfers between devices with their start and end apart: 93, of which 36 were waited for; matrix products, arithmetic and copies ran while one was open for 3% of the time, Pallas kernels for 15%

profile of v3, /device:TPU:0, one launch (start us, length us, event | category | flops | bytes accessed | tf_op | source)
XLA Modules:
  0.0 566.5 jit_solution(16580227054609844988)
XLA Ops:
  19.5 8.3 %collective-permute-done.refs_3_.refs_1_ = bf16[256,512]{1,0:T(8,128)(2,1)} collective-permute-done((bf16[256,512]{1,0:T(8,128)(2,1)}, bf16[256,512]{1,0:T(8,128)(2,1)}, u32[]{:S(2)}, u32[]{:S(2)}) %collective-permute-start) | collective-permute-done | bytes 262176 | tf_op jit(solution)/shard_map/ppermute | solution.py:48
  40.5 6.3 %norm1.1 = (bf16[512,2048]{1,0:T(8,128)(2,1)S(1)}, f32[512,1]{1,0:T(8,128)S(1)}, f32[512,1]{1,0:T(8,128)S(1)}, bf16[512,512]{1,0:T(8,128)(2,1)}) custom-call(s32[8]{0:T(128)S(1)} %stack.35.refs_0_, bf16[256,512]{1,0:T(8,128)(2,1)} %get-tuple-element.224.refs_1_, bf16[256,512]{1,0:T(8,128)(2,1)S(1)} %get-tuple-element.223.refs_2_, ...), custom_call_target="tpu_custom_call" | custom-call | flops 5500000256 | tf_op jit(solution)/shard_map/norm1/pallas_call | solution.py:129
  56.3 5.4 key_value.1
  105.6 5.4 mix.1
  156.5 10.1 %feed_up.1 = (bf16[512,2048]{1,0:T(8,128)(2,1)S(1)}, f32[512,1]{1,0:T(8,128)S(1)}, f32[512,1]{1,0:T(8,128)S(1)}, f32[512,512]{1,0:T(8,128)S(1)}, bf16[512,1024]{...) custom-call(s32[8]{0:T(128)S(1)} %stack.35.refs_0_, bf16[256,512]{1,0:T(8,128)(2,1)} %get-tuple-element.224.refs_1_, ...), custom_call_target="tpu_custom_call" | custom-call | flops 12099999744 | tf_op jit(solution)/shard_map/feed_up/pallas_call | solution.py:129
  166.6 5.9 %back_feed.1 = (bf16[272,512]{1,0:T(8,128)(2,1)S(1)}, bf16[256,512]{1,0:T(8,128)(2,1)S(1)}, bf16[272,512]{1,0:T(8,128)(2,1)S(1)}, bf16[256,512]{1,0:T(8,128)(2,1...) custom-call(s32[8]{0:T(128)S(1)} %stack.35.refs_0_, ...), custom_call_target="tpu_custom_call" | custom-call | flops 7699999744 | tf_op jit(solution)/shard_map/back_feed/pallas_call | solution.py:129
  194.4 7.1 %collective-permute-done.31.refs_3_ = bf16[256,512]{1,0:T(8,128)(2,1)S(1)} collective-permute-done((bf16[256,512]{1,0:T(8,128)(2,1)S(1)}, bf16[256,512]{1,0:T(8,128)(2,1)S(1)}, u32[]{:S(2)}, u32[]{:S(2)}) %collective-permute-start.31) | collective-permute-done | bytes 262176 | tf_op jit(solution)/shard_map/ppermute | solution.py:48
  202.3 6.8 %collective-permute-done.34.refs_5_ = bf16[256,512]{1,0:T(8,128)(2,1)} collective-permute-done((bf16[256,512]{1,0:T(8,128)(2,1)}, bf16[256,512]{1,0:T(8,128)(2,1)}, u32[]{:S(2)}, u32[]{:S(2)}) %collective-permute-start.34) | collective-permute-done | bytes 262176 | tf_op jit(solution)/shard_map/ppermute | solution.py:52
  221.1 7.4 %collective-permute-done.35.refs_3_ = bf16[256,512]{1,0:T(8,128)(2,1)S(1)} collective-permute-done((bf16[256,512]{1,0:T(8,128)(2,1)}, bf16[256,512]{1,0:T(8,128)(2,1)S(1)}, u32[]{:S(2)}, u32[]{:S(2)}) %collective-permute-start.35) | collective-permute-done | bytes 262176 | tf_op jit(solution)/shard_map/ppermute | solution.py:48
  232.2 4.6 w2_own.1.refs_5_.refs_15_
  239.3 4.7 w1_own.1.refs_16_
  249.1 6.5 %back_mix.1 = (bf16[512,2048]{1,0:T(8,128)(2,1)S(1)}, bf16[512,1024]{1,0:T(8,128)(2,1)S(1)}, bf16[512,1024]{1,0:T(8,128)(2,1)S(1)}, f32[256,512]{1,0:T(8,128)S(1)}, bf16[256,512]{1,0:T(8,128)(2,1)S(1)}) custom-call(s32[8]{0:T(128)S(1)} %stack.35.refs_0_, bf16[256,512]{1,0:T(8,128)(2,1)} %get-tuple-element.161.refs_1_, ...), custom_call_target="tpu_custom_call" | custom-call | flops 8800000000 | tf_op jit(solution)/shard_map/back_mix/pallas_call | solution.py:129
  322.0 10.1 %back_proj.1 = (bf16[272,512]{1,0:T(8,128)(2,1)S(1)}, bf16[256,512]{1,0:T(8,128)(2,1)S(1)}, bf16[272,512]{1,0:T(8,128)(2,1)S(1)}, bf16[256,512]{1,0:T(8,128)(2,1...) custom-call(s32[8]{0:T(128)S(1)} %stack.35.refs_0_, ...), custom_call_target="tpu_custom_call" | custom-call | flops 13200000000 | tf_op jit(solution)/shard_map/back_proj/pallas_call | solution.py:129
  334.2 6.4 %collective-permute-done.58 = bf16[256,512]{1,0:T(8,128)(2,1)S(1)} collective-permute-done((bf16[256,512]{1,0:T(8,128)(2,1)S(1)}, bf16[256,512]{1,0:T(8,128)(2,1)S(1)}, u32[]{:S(2)}, u32[]{:S(2)}) %collective-permute-start.58) | collective-permute-done | bytes 262176 | tf_op jit(solution)/shard_map/ppermute | solution.py:52
  343.4 4.7 wo_own.1.refs_6_.refs_11_
  348.2 5.9 %collective-permute-done.61.refs_3_ = bf16[1024,1536]{1,0:T(8,128)(2,1)S(1)} collective-permute-done((bf16[1024,1536]{1,0:T(8,128)(2,1)}, bf16[1024,1536]{1,0:T(8,128)(2,1)S(1)}, u32[]{:S(2)}, u32[]{:S(2)}) %collective-permute-start.61) | collective-permute-done | bytes 3145760 | tf_op jit(solution)/shard_map/ppermute | solution.py:1109
  369.6 5.0 wv_own.1
  383.2 5.5 reduce-scatter.16.cloned.1.call-done
  408.2 18.9 %collective-permute-done.66 = f32[2,512]{1,0:T(2,128)S(1)} collective-permute-done((f32[2,512]{1,0:T(2,128)S(1)}, f32[2,512]{1,0:T(2,128)S(1)}, u32[]{:S(2)}, u32[]{:S(2)}) %collective-permute-start.66) | collective-permute-done | bytes 4128 | tf_op jit(solution)/shard_map/ppermute | solution.py:979
  429.9 28.8 %reduce-scatter.12.cloned.1.call-done = bf16[256,1536]{1,0:T(8,128)(2,1)} async-done(((bf16[1024,1536]{1,0:T(8,128)(2,1)}), bf16[256,1536]{1,0:T(8,128)(2,1)}) %reduce-scatter.12.cloned.1.call-update) | async-done | bytes 786448 | tf_op jit(solution)/shard_map/reduce_scatter | solution.py:828
  478.5 6.9 %reduce-scatter.22.cloned.1.call-done = bf16[64,1024]{1,0:T(8,128)(2,1)} async-done(((bf16[256,1024]{1,0:T(8,128)(2,1)}), bf16[64,1024]{1,0:T(8,128)(2,1)}) %reduce-scatter.22.cloned.1.call-update) | async-done | bytes 131088 | tf_op jit(solution)/shard_map/reduce_scatter | solution.py:828
  494.8 13.3 %reduce-scatter.26.cloned.1.call-done = bf16[64,1024]{1,0:T(8,128)(2,1)} async-done(((bf16[256,1024]{1,0:T(8,128)(2,1)}), bf16[64,1024]{1,0:T(8,128)(2,1)}) %reduce-scatter.26.cloned.1.call-update) | async-done | bytes 131088 | tf_op jit(solution)/shard_map/reduce_scatter | solution.py:828
  510.5 21.1 %reduce-scatter.18.cloned.1.call-done = bf16[64,1024]{1,0:T(8,128)(2,1)} async-done(((bf16[256,1024]{1,0:T(8,128)(2,1)}), bf16[64,1024]{1,0:T(8,128)(2,1)}) %reduce-scatter.18.cloned.1.call-update) | async-done | bytes 131088 | tf_op jit(solution)/shard_map/reduce_scatter | solution.py:828
  533.2 22.9 %reduce-scatter.14.cloned.1.call-done = bf16[64,1536]{1,0:T(8,128)(2,1)} async-done(((bf16[256,1536]{1,0:T(8,128)(2,1)}), bf16[64,1536]{1,0:T(8,128)(2,1)}) %reduce-scatter.14.cloned.1.call-update) | async-done | bytes 196624 | tf_op jit(solution)/shard_map/reduce_scatter | solution.py:828
  (543 shorter events, 320.9 us)
Async XLA Ops:
  7.2 91.4 %all-gather.2.cloned.1.call-start = ((), (), s32[]{:S(2)}) async-start(), calls=%async_computation.9 | async-start | bytes 2621440 | tf_op jit(solution)/shard_map/all_gather | solution.py:1032
  13.1 23.4 %collective-permute-start.5 = (bf16[256,512]{1,0:T(8,128)(2,1)}, bf16[256,512]{1,0:T(8,128)(2,1)}, u32[]{:S(2)}, u32[]{:S(2)}) collective-permute-start(bf16[256,512]{1,0:T(8,128)(2,1)} %get-tuple-element.224.refs_1_), channel_id=1, source_target_pairs={{0,3},{1,0},{2,1},{3,2},{4,7},{5,4},{6,5},{7,6},{8,11},{9,8},{10,9... | collective-permute-start | bytes 786440 | tf_op jit(solution)/shard_map/ppermute | solution.py:52
  49.7 256.2 %reduce-scatter.10.cloned.1.call-start = ((), (), s32[]{:S(2)}) async-start(), calls=%async_computation.10 | async-start | bytes 2621440 | tf_op jit(solution)/shard_map/reduce_scatter | solution.py:1108
  186.9 43.7 %collective-permute-start.41 = (bf16[1024,1024]{1,0:T(8,128)(2,1)}, bf16[1024,1024]{1,0:T(8,128)(2,1)}, u32[]{:S(2)}, u32[]{:S(2)}) collective-permute-start(bf16[1024,1024]{1,0:T(8,128)(2,1)} %w2_other.1.refs_4_.refs_12_), channel_id=1, source_target_pairs={{0,4},{4,0},{8,12},{12,8},{16,20},{20,16},{24,28},{28,24},{32,36},... | collective-permute-start | bytes 6291464 | tf_op jit(solution)/shard_map/ppermute | solution.py:1070
  190.6 46.3 %collective-permute-start.42 = (bf16[1024,1024]{1,0:T(8,128)(2,1)S(1)}, bf16[1024,1024]{1,0:T(8,128)(2,1)}, u32[]{:S(2)}, u32[]{:S(2)}) collective-permute-start(bf16[1024,1024]{1,0:T(8,128)(2,1)S(1)} %w1_other.1.refs_11_), channel_id=1, source_target_pairs={{0,4},{4,0},{8,12},{12,8},{16,20},{20,16},{24,28},{28,24},{32,36},... | collective-permute-start | bytes 6291464 | tf_op jit(solution)/shard_map/ppermute | solution.py:1070
  265.1 94.6 %reduce-scatter.20.cloned.1.call-start = ((), (), s32[]{:S(2)}) async-start(), calls=%async_computation.15 | async-start | bytes 2621440 | tf_op jit(solution)/shard_map/reduce_scatter | solution.py:828
  265.8 94.9 %reduce-scatter.24.cloned.1.call-start = ((), (), s32[]{:S(2)}) async-start(), calls=%async_computation.17 | async-start | bytes 2621440 | tf_op jit(solution)/shard_map/reduce_scatter | solution.py:828
  270.7 118.0 %reduce-scatter.16.cloned.1.call-start = ((), (), s32[]{:S(2)}) async-start(), calls=%async_computation.13 | async-start | bytes 2621440 | tf_op jit(solution)/shard_map/reduce_scatter | solution.py:828
  294.0 49.4 %collective-permute-start.60 = (bf16[1024,1024]{1,0:T(8,128)(2,1)}, bf16[1024,1024]{1,0:T(8,128)(2,1)}, u32[]{:S(2)}, u32[]{:S(2)}) collective-permute-start(bf16[1024,1024]{1,0:T(8,128)(2,1)} %wo_other.1.refs_8_), channel_id=1, source_target_pairs={{0,4},{4,0},{8,12},{12,8},{16,20},{20,16},{24,28},{28,24},{32,36},... | collective-permute-start | bytes 6291464 | tf_op jit(solution)/shard_map/ppermute | solution.py:1109
  348.1 110.5 %reduce-scatter.12.cloned.1.call-start = ((), (), s32[]{:S(2)}) async-start(), calls=%async_computation.11 | async-start | bytes 3932160 | tf_op jit(solution)/shard_map/reduce_scatter | solution.py:828
  359.4 126.0 %reduce-scatter.22.cloned.1.call-start = ((), (), s32[]{:S(2)}) async-start(), calls=%async_computation.16 | async-start | bytes 655360 | tf_op jit(solution)/shard_map/reduce_scatter | solution.py:828
  360.1 148.0 %reduce-scatter.26.cloned.1.call-start = ((), (), s32[]{:S(2)}) async-start(), calls=%async_computation.18 | async-start | bytes 655360 | tf_op jit(solution)/shard_map/reduce_scatter | solution.py:828
  360.9 170.7 %reduce-scatter.18.cloned.1.call-start = ((), (), s32[]{:S(2)}) async-start(), calls=%async_computation.14 | async-start | bytes 655360 | tf_op jit(solution)/shard_map/reduce_scatter | solution.py:828
  361.0 27.7 %collective-permute-start.57 = (bf16[272,512]{1,0:T(8,128)(2,1)S(1)}, bf16[272,512]{1,0:T(8,128)(2,1)}, u32[]{:S(2)}, u32[]{:S(2)}) collective-permute-start(bf16[272,512]{1,0:T(8,128)(2,1)S(1)} %get-tuple-element.195), channel_id=1, source_target_pairs={{0,3},{1,0},{2,1},{3,2},{4,7},{5,4},{6,5},{7,6},{8,11},{9,8},{10,9... | collective-permute-start | bytes 835592 | tf_op jit(solution)/shard_map/ppermute | solution.py:52
  361.0 27.7 %collective-permute-start.56 = (bf16[256,512]{1,0:T(8,128)(2,1)}, bf16[256,512]{1,0:T(8,128)(2,1)}, u32[]{:S(2)}, u32[]{:S(2)}) collective-permute-start(bf16[256,512]{1,0:T(8,128)(2,1)} %get-tuple-element.194), channel_id=1, source_target_pairs={{0,1},{1,2},{2,3},{3,0},{4,5},{5,6},{6,7},{7,4},{8,9},{9,10},{10,1... | collective-permute-start | bytes 786440 | tf_op jit(solution)/shard_map/ppermute | solution.py:48
  363.0 25.7 %collective-permute-start.59 = (bf16[256,512]{1,0:T(8,128)(2,1)S(1)}, bf16[256,512]{1,0:T(8,128)(2,1)}, u32[]{:S(2)}, u32[]{:S(2)}) collective-permute-start(bf16[256,512]{1,0:T(8,128)(2,1)S(1)} %add_convert_fusion.3.refs_4_.refs_5_), channel_id=1, source_target_pairs={{0,3},{1,0},{2,1},{3,2},{4,7},{5,4},{6,5},{7,6},{8,11},{9,8},{10,9... | collective-permute-start | bytes 786440 | tf_op jit(solution)/shard_map/ppermute | solution.py:52
  364.3 24.4 %collective-permute-start.55 = (bf16[272,512]{1,0:T(8,128)(2,1)S(1)}, bf16[272,512]{1,0:T(8,128)(2,1)}, u32[]{:S(2)}, u32[]{:S(2)}) collective-permute-start(bf16[272,512]{1,0:T(8,128)(2,1)S(1)} %add_convert_fusion.1.refs_3_.refs_4_), channel_id=1, source_target_pairs={{0,1},{1,2},{2,3},{3,0},{4,5},{5,6},{6,7},{7,4},{8,9},{9,10},{10,1... | collective-permute-start | bytes 835592 | tf_op jit(solution)/shard_map/ppermute | solution.py:48
  388.7 167.4 %reduce-scatter.14.cloned.1.call-start = ((), (), s32[]{:S(2)}) async-start(), calls=%async_computation.12 | async-start | bytes 983040 | tf_op jit(solution)/shard_map/reduce_scatter | solution.py:828
  399.6 59.1 %collective-permute-start.71 = (bf16[256,512]{1,0:T(8,128)(2,1)}, bf16[256,512]{1,0:T(8,128)(2,1)S(1)}, u32[]{:S(2)}, u32[]{:S(2)}) collective-permute-start(bf16[256,512]{1,0:T(8,128)(2,1)} %get-tuple-element.203.refs_14_), channel_id=1, source_target_pairs={{0,64},{4,68},{8,72},{12,76},{16,80},{20,84},{24,88},{28,92},{32,9... | collective-permute-start | bytes 786440 | tf_op jit(solution)/shard_map/ppermute | solution.py:871
  402.3 58.9 %collective-permute-start.72 = (bf16[256,512]{1,0:T(8,128)(2,1)}, bf16[256,512]{1,0:T(8,128)(2,1)S(1)}, u32[]{:S(2)}, u32[]{:S(2)}) collective-permute-start(bf16[256,512]{1,0:T(8,128)(2,1)} %get-tuple-element.208), channel_id=1, source_target_pairs={{0,32},{4,36},{8,40},{12,44},{16,48},{20,52},{24,56},{28,60},{32,6... | collective-permute-start | bytes 786440 | tf_op jit(solution)/shard_map/ppermute | solution.py:871
  402.3 61.8 %collective-permute-start.73 = (bf16[256,512]{1,0:T(8,128)(2,1)S(1)}, bf16[256,512]{1,0:T(8,128)(2,1)S(1)}, u32[]{:S(2)}, u32[]{:S(2)}) collective-permute-start(bf16[256,512]{1,0:T(8,128)(2,1)S(1)} %copy-done.62), channel_id=1, source_target_pairs={{0,96},{4,100},{8,104},{12,108},{16,112},{20,116},{24,120},{28,124... | collective-permute-start | bytes 786440 | tf_op jit(solution)/shard_map/ppermute | solution.py:871
  405.6 24.3 %collective-permute-start.67 = (f32[2,512]{1,0:T(2,128)S(1)}, f32[2,512]{1,0:T(2,128)S(1)}, u32[]{:S(2)}, u32[]{:S(2)}) collective-permute-start(f32[2,512]{1,0:T(2,128)S(1)} %fusion.13), channel_id=1, source_target_pairs={{0,96},{4,100},{8,104},{12,108},{16,112},{20,116},{24,120},{28,124... | collective-permute-start | bytes 12296 | tf_op jit(solution)/shard_map/ppermute | solution.py:979
  427.1 59.9 %collective-permute-start.77 = (bf16[256,1024]{1,0:T(8,128)(2,1)}, bf16[256,1024]{1,0:T(8,128)(2,1)S(1)}, u32[]{:S(2)}, u32[]{:S(2)}) collective-permute-start(bf16[256,1024]{1,0:T(8,128)(2,1)} %get-tuple-element.202.refs_6_.refs_13_), channel_id=1, source_target_pairs={{0,64},{4,68},{8,72},{12,76},{16,80},{20,84},{24,88},{28,92},{32,9... | collective-permute-start | bytes 1572872 | tf_op jit(solution)/shard_map/ppermute | solution.py:871
  429.8 57.1 %collective-permute-start.78 = (bf16[256,1024]{1,0:T(8,128)(2,1)S(1)}, bf16[256,1024]{1,0:T(8,128)(2,1)S(1)}, u32[]{:S(2)}, u32[]{:S(2)}) collective-permute-start(bf16[256,1024]{1,0:T(8,128)(2,1)S(1)} %copy-done.54), channel_id=1, source_target_pairs={{0,32},{4,36},{8,40},{12,44},{16,48},{20,52},{24,56},{28,60},{32,6... | collective-permute-start | bytes 1572872 | tf_op jit(solution)/shard_map/ppermute | solution.py:871
  (205 other events, 1505.4 us)
Sparse Core Ops, SparseCore 0:
  49.8 32.3 all-gather.1
  265.2 28.1 reduce-scatter.9
  295.9 29.2 reduce-scatter.19
  327.4 29.3 reduce-scatter.23
  359.2 29.4 reduce-scatter.15
  390.9 67.6 reduce-scatter.11
  461.0 24.2 reduce-scatter.21
  487.7 20.3 reduce-scatter.25
  510.5 21.0 reduce-scatter.17
  533.8 22.2 reduce-scatter.13
